TPU v7x, 32 devices: a whole 2x2x4 slice. The times are simulated.
32 devices in a mesh: kx: 2 (over core), ky: 4 (over y, x), kz: 4 (over z).
Axes of the slice: x: 2, y: 2, z: 4, core: 2. Of those that a mesh axis runs over, the one named last changes fastest.
Arguments:
- populations: float32 [16, 8, 4, 64, 64], P('kx', None, None, 'ky', 'kz'), may hold values from -6 to 6
- force: float32 [16, 3, 4, 64, 64], P('kx', None, None, 'ky', 'kz'), may hold values from -3 to 3
- rate: float32 [16, 4, 64, 64], P('kx', None, 'ky', 'kz'), may hold values from 0.05 to 0.5
- tiles: bfloat16 [4, 1024, 1024], replicated, may hold values from -0.1875 to 0.1875
- send_planes: int32 [2, 4, 4, 4, 2], P('kx', 'ky', 'kz'), may hold values from 0 to 7
- recv_target: int32 [2, 4, 4, 4, 2], P('kx', 'ky', 'kz'), may hold values from 0 to 7
- recv_tile: int32 [2, 4, 4, 4, 2], P('kx', 'ky', 'kz'), may hold values from 0 to 3
- recv_count: int32 [2, 4, 4, 4], P('kx', 'ky', 'kz'), may hold values from 0 to 2, as said below
Outputs:
- final_populations: float32 [16, 8, 4, 64, 64], P('kx', None, None, 'ky', 'kz')
Inputs may be any that keep to these rules, and one draw needn't show every extreme that they name: `recv_count`: every receiving brick has some source brick with all 2 slots valid, and some receiving brick has all 2 slots valid from every source brick.
All inputs are finite; a program needn't handle non-finite values.
Results may differ from a plain program's by a relative error of at most 0.0042.
Values may be sent and summed in bfloat16 or wider, within the bound.
A program may use at most 128 MiB of HBM per device.

v0:
```python
import jax
import jax.numpy as jnp
from jax import lax
from jax.sharding import PartitionSpec as P

ITERS = 2


def extended(x, sides, width):
    for axis, dim in sides:
        size, length = (lax.axis_size(axis), x.shape[dim])
        up = [(i, (i + 1) % size) for i in range(size)]
        down = [(j, i) for i, j in up]
        last = lax.slice_in_dim(x, length - width, length, axis=dim)
        leading = lax.slice_in_dim(x, 0, width, axis=dim)
        before = lax.ppermute(last, axis, up)
        after = lax.ppermute(leading, axis, down)
        x = jnp.concatenate([before, x, after], axis=dim)
    return x


def centered(padded, along, length):

    def window(offset):
        return lax.slice_in_dim(padded, offset, offset + length, axis=along)

    return (8.0 * (window(3) - window(1)) - (window(4) - window(0))) / 12.0


def per_device(populations, force, rate, tiles, send_planes, recv_target, recv_tile, recv_count):
    width_x, drive_count, band_count, width_y, width_z = populations.shape
    block_len = band_count * width_y * width_z
    peer_count = lax.axis_size("kz")
    slot_cap = send_planes.shape[-1]
    tile_count = tiles.shape[0]
    plane_list = send_planes.reshape(peer_count * slot_cap)
    slot_count = recv_count.reshape(peer_count)
    target_ids = recv_target.reshape(peer_count, slot_cap)
    tile_ids = recv_tile.reshape(peer_count, slot_cap)
    usable = lax.broadcasted_iota(jnp.int32, (peer_count, slot_cap), 1) < slot_count[:, None]
    tile_match = (
        tile_ids[None, None] == jnp.arange(tile_count, dtype=jnp.int32)[:, None, None, None]
    )
    plane_match = (
        target_ids[None, None] == jnp.arange(width_x, dtype=jnp.int32)[None, :, None, None]
    )
    selector = (tile_match & plane_match & usable[None, None]).astype(jnp.bfloat16)
    selector = selector.reshape(tile_count * width_x, peer_count * slot_cap)
    force_x = force[:, 0][:, None]
    force_y = force[:, 1][:, None]
    force_z = force[:, 2][:, None]
    rate_wide = rate[:, None]
    current = populations
    for iteration in range(ITERS):
        x_padded = extended(current, (("kx", 0),), 2)
        y_padded = extended(current, (("ky", 3),), 2)
        z_padded = extended(current, (("kz", 4),), 2)
        drift_term = force_x * centered(x_padded, 0, width_x)
        drift_term = drift_term + force_y * centered(y_padded, 3, width_y)
        drift_term = drift_term + force_z * centered(z_padded, 4, width_z)
        rounded = current.astype(jnp.bfloat16)
        plane_rows = rounded.reshape(width_x, drive_count, block_len)
        outgoing = plane_rows[plane_list].reshape(peer_count, slot_cap, drive_count, block_len)
        incoming = lax.all_to_all(outgoing, "kz", split_axis=0, concat_axis=0, tiled=True)
        summed = jnp.dot(
            selector,
            incoming.reshape(peer_count * slot_cap, drive_count * block_len),
            preferred_element_type=jnp.float32,
        )
        grouped = summed.astype(jnp.bfloat16).reshape(tile_count, width_x * drive_count, block_len)
        collision = jnp.einsum("tmk,tlk->ml", grouped, tiles, preferred_element_type=jnp.float32)
        collision = collision.reshape(width_x, drive_count, band_count, width_y, width_z)
        current = current - drift_term + collision - rate_wide * current
    return current


def solution(mesh):
    placed = (
        P("kx", None, None, "ky", "kz"),
        P("kx", None, None, "ky", "kz"),
        P("kx", None, "ky", "kz"),
        P(),
        P("kx", "ky", "kz", None, None),
        P("kx", "ky", "kz", None, None),
        P("kx", "ky", "kz", None, None),
        P("kx", "ky", "kz", None),
    )
    return jax.shard_map(
        per_device,
        mesh=mesh,
        in_specs=placed,
        out_specs=P("kx", None, None, "ky", "kz"),
        check_vma=False,
    )
```

profile of v0, /device:TPU:0, one launch (start us, length us, event | category | flops | bytes accessed | tf_op | source)
XLA Modules:
  0.0 136.8 jit_solution(7362803941651458464)
XLA Ops:
  0.0 2.8 %copy.66 = f32[8,8,4,16,16]{4,1,3,2,0:T(8,128)S(1)} copy(f32[8,8,4,16,16]{4,3,2,1,0:T(8,128)} %param.8) | data formatting | bytes 524288 | tf_op args[0]
  2.8 0.0 copy-start.1
  2.8 0.0 copy-start
  2.8 1.1 fusion.54
  3.9 0.5 collective-permute-start.1
  4.3 0.1 copy-done.1
  4.5 0.8 fusion.55
  5.3 2.9 %collective-permute-start.3 = (f32[8,8,4,2,16]{4,1,3,2,0:T(8,128)}, f32[8,8,4,2,16]{4,1,3,2,0:T(8,128)}, u32[]{:S(2)}, u32[]{:S(2)}) collective-permute-start(f32[8,8,4,2,16]{4,1,3,2,0:T(8,128)} %get-tuple-element.18), channel_id=1, source_target_pairs={{0,4},{4,8},{8,12},{12,0},{1,5},{5,9},{9,13},{13,1},{2,6},{6,10},{... | collective-permute-start | bytes 98312 | tf_op jit(solution)/shard_map/ppermute | solution.py:16
  8.2 0.2 convert_element_type.13
  8.5 0.1 copy.69
  8.6 0.1 reshape.165
  8.7 1.8 %reshape.164 = bf16[8,8,1024]{2,1,0:T(8,128)(2,1)S(1)} reshape(bf16[8,8,4,16,16]{4,3,2,1,0:T(8,128)(2,1)S(1)} %convert_element_type.13) | data formatting | bytes 262144 | tf_op jit(solution)/shard_map/reshape | solution.py:62
  10.4 1.2 gather_fusion
  11.6 4.9 %all-to-all-start = ((bf16[4,2,8,1024]{3,2,1,0:T(8,128)(2,1)}), bf16[4,2,8,1024]{3,2,1,0:T(8,128)(2,1)S(1)}, u32[]{:S(2)}, u32[]{:S(2)}) async-start(bf16[4,2,8,1024]{3,2,1,0:T(8,128)(2,1)} %bitcast.7), calls=%async_computation | async-start | bytes 262144 | tf_op jit(solution)/shard_map/all_to_all | solution.py:64
  16.5 2.8 %fusion.56 = (f32[8,8,4,16,2]{4,3,2,1,0:T(8,128)}, f32[8,8,4,16,2]{4,3,2,1,0:T(8,128)}) fusion(f32[8,8,4,16,16]{4,3,2,1,0:T(8,128)S(1)} %copy-done), kind=kLoop, calls=%fused_computation.95 | loop fusion | bytes 131072 | tf_op jit(solution)/shard_map/slice | solution.py:15
  19.3 3.9 %copy.89 = f32[8,8,4,16,2]{3,1,4,2,0:T(8,128)} copy(f32[8,8,4,16,2]{4,3,2,1,0:T(8,128)} %get-tuple-element.19) | data formatting | bytes 65536
  23.2 3.8 %collective-permute-start.4 = (f32[8,8,4,16,2]{3,1,4,2,0:T(8,128)}, f32[8,8,4,16,2]{3,1,4,2,0:T(8,128)S(1)}, u32[]{:S(2)}, u32[]{:S(2)}) collective-permute-start(f32[8,8,4,16,2]{3,1,4,2,0:T(8,128)} %copy.89), channel_id=1, source_target_pairs={{1,0},{2,1},{3,2},{0,3},{5,4},{6,5},{7,6},{4,7},{9,8},{10,9},{11,1... | collective-permute-start | bytes 98312 | tf_op jit(solution)/shard_map/ppermute | solution.py:17
  27.1 3.1 %copy.90 = f32[8,8,4,16,2]{3,1,4,2,0:T(8,128)S(1)} copy(f32[8,8,4,16,2]{4,3,2,1,0:T(8,128)} %get-tuple-element.20) | data formatting | bytes 65536
  30.2 0.0 collective-permute-start.5
  30.3 0.9 multiply_bitcast_fusion.2
  31.2 0.1 copy.68
  31.3 0.1 iota_compare_fusion
  31.3 0.1 copy.67
  31.4 0.1 iota_compare_fusion.1
  31.5 0.1 iota_compare_fusion.2
  31.6 0.1 and_and_fusion
  31.7 0.1 and.52
  31.8 2.3 %collective-permute-done.4 = f32[8,8,4,16,2]{3,1,4,2,0:T(8,128)S(1)} collective-permute-done((f32[8,8,4,16,2]{3,1,4,2,0:T(8,128)}, f32[8,8,4,16,2]{3,1,4,2,0:T(8,128)S(1)}, u32[]{:S(2)}, u32[]{:S(2)}) %collective-permute-start.4) | collective-permute-done | bytes 32800 | tf_op jit(solution)/shard_map/ppermute | solution.py:17
  34.1 1.4 %collective-permute-start.2 = (f32[8,8,4,2,16]{4,1,3,2,0:T(8,128)}, f32[8,8,4,2,16]{4,1,3,2,0:T(8,128)S(1)}, u32[]{:S(2)}, u32[]{:S(2)}) collective-permute-start(f32[8,8,4,2,16]{4,1,3,2,0:T(8,128)} %get-tuple-element.17), channel_id=1, source_target_pairs={{4,0},{8,4},{12,8},{0,12},{5,1},{9,5},{13,9},{1,13},{6,2},{10,6},{... | collective-permute-start | bytes 98312 | tf_op jit(solution)/shard_map/ppermute | solution.py:17
  35.5 2.9 %copy.62 = f32[8,8,4,16,2]{4,1,3,2,0:T(8,128)} copy(f32[8,8,4,16,2]{3,1,4,2,0:T(8,128)S(1)} %collective-permute-done.4) | data formatting | bytes 65536 | tf_op jit(solution)/shard_map/ppermute | solution.py:17
  38.4 1.6 %collective-permute-done.5 = f32[8,8,4,16,2]{3,1,4,2,0:T(8,128)} collective-permute-done((f32[8,8,4,16,2]{3,1,4,2,0:T(8,128)S(1)}, f32[8,8,4,16,2]{3,1,4,2,0:T(8,128)}, u32[]{:S(2)}, u32[]{:S(2)}) %collective-permute-start.5) | collective-permute-done | bytes 32800 | tf_op jit(solution)/shard_map/ppermute | solution.py:16
  40.0 3.8 %copy.64 = f32[8,8,4,16,2]{4,1,3,2,0:T(8,128)} copy(f32[8,8,4,16,2]{3,1,4,2,0:T(8,128)} %collective-permute-done.5) | data formatting | bytes 65536 | tf_op jit(solution)/shard_map/ppermute | solution.py:16
  43.8 1.0 constant_dynamic-update-slice_fusion.7
  44.8 1.1 constant_dynamic-update-slice_fusion.3
  45.9 4.0 %constant_dynamic-update-slice_fusion.1 = (f32[10,8,4,16,16]{4,1,3,2,0:T(8,128)}, f32[10,8,4,16,16]{4,1,3,2,0:T(8,128)S(1)}, f32[8,8,4,18,16]{4,1,3,2,0:T(8,128)}, f32[8,8,4,18,16]{4,1,3,2,0:T(8,128)S(1)}) fusion(f32[8,8,4,16,16]{4,3,2,1,0:T(8,128)S(1)} %copy-done, f32[10,8,4,16,16]{4,1,3,2,0:T(8,128)S(1)} %constant_dynamic-update-slice_fusion.3, ...), kind=kLoop, calls=%fused_computation.76 | loop fusion | bytes 10485760
  49.9 0.8 constant_dynamic-update-slice_fusion.4
  50.7 0.8 copy-done.7
  51.4 0.8 copy-done.8
  52.2 1.9 %constant_dynamic-update-slice_fusion = f32[10,8,4,16,16]{4,1,3,2,0:T(8,128)} fusion(f32[10,8,4,16,16]{4,1,3,2,0:T(8,128)} %get-tuple-element.13, f32[2,8,4,16,16]{4,1,3,2,0:T(8,128)} %collective-permute-done), kind=kLoop, calls=%fused_computation.75 | loop fusion | bytes 1048576 | tf_op jit(solution)/shard_map/concatenate | solution.py:18
  54.1 0.1 copy.91
  54.2 0.3 convolution_convert_fusion.1
  54.5 0.2 reshape.168
  54.8 22.3 %fusion.57 = (bf16[8,8,4,16,16]{4,1,3,2,0:T(8,128)(2,1)}, f32[8,8,4,16,16]{4,1,3,2,0:T(8,128)S(1)}) fusion(f32[8,8,4,16,16]{4,1,3,2,0:T(8,128)} %copy-done.1, f32[8,4,16,16]{3,2,1,0:T(8,128)} %param.10, bf16[4,16,16,1024,4]{3,2,1,0,4:T(8,128)(2,1)} %bitcast.72, f32[8,4,16,16]{3,2,1,0:T(8,128)S(1)} %copy-done.5, f32[8,8,4,16,2]{4,1,3,2,0:T(8,128)} %copy.64, ...), kind=kOutput, calls=%fused_computation.96 | convolution fusion | flops 538574848 | bytes 11862016 | tf_op jit(solution)/shard_map/tmk,tlk->ml/dot_general | solution.py:71
  77.1 2.7 %fusion.51 = (f32[8,8,4,16,2]{4,1,3,2,0:T(8,128)}, f32[8,8,4,16,2]{4,1,3,2,0:T(8,128)}) fusion(f32[8,8,4,16,16]{4,1,3,2,0:T(8,128)S(1)} %get-tuple-element.25), kind=kLoop, calls=%fused_computation.90 | loop fusion | bytes 131072 | tf_op jit(solution)/shard_map/slice | solution.py:15
  79.8 1.1 fusion.52
  80.9 3.9 %copy.73 = f32[8,8,4,16,2]{3,1,4,2,0:T(8,128)} copy(f32[8,8,4,16,2]{4,1,3,2,0:T(8,128)} %get-tuple-element.5) | data formatting | bytes 65536 | tf_op jit(solution)/shard_map/slice | solution.py:15
  84.8 2.9 %collective-permute-start.10 = (f32[8,8,4,16,2]{3,1,4,2,0:T(8,128)}, f32[8,8,4,16,2]{3,1,4,2,0:T(8,128)S(1)}, u32[]{:S(2)}, u32[]{:S(2)}) collective-permute-start(f32[8,8,4,16,2]{3,1,4,2,0:T(8,128)} %copy.73), channel_id=1, source_target_pairs={{1,0},{2,1},{3,2},{0,3},{5,4},{6,5},{7,6},{4,7},{9,8},{10,9},{11,1... | collective-permute-start | bytes 98312 | tf_op jit(solution)/shard_map/ppermute | solution.py:17
  87.7 3.9 %copy.75 = f32[8,8,4,16,2]{3,1,4,2,0:T(8,128)} copy(f32[8,8,4,16,2]{4,1,3,2,0:T(8,128)} %get-tuple-element.6) | data formatting | bytes 65536 | tf_op jit(solution)/shard_map/slice | solution.py:14
  91.6 1.5 %copy.77 = bf16[8,8,4,16,16]{4,3,2,1,0:T(8,128)(2,1)S(1)} copy(bf16[8,8,4,16,16]{4,1,3,2,0:T(8,128)(2,1)} %get-tuple-element.24) | data formatting | bytes 262144 | tf_op jit(solution)/shard_map/convert_element_type | solution.py:61
  93.1 1.8 %reshape.169 = bf16[8,8,1024]{2,1,0:T(8,128)(2,1)S(1)} reshape(bf16[8,8,4,16,16]{4,3,2,1,0:T(8,128)(2,1)S(1)} %copy.77) | data formatting | bytes 262144 | tf_op jit(solution)/shard_map/reshape | solution.py:62
  94.8 1.2 gather_fusion.1
  96.1 5.1 %all-to-all-start.1 = ((bf16[4,2,8,1024]{3,2,1,0:T(8,128)(2,1)}), bf16[4,2,8,1024]{3,2,1,0:T(8,128)(2,1)S(1)}, u32[]{:S(2)}, u32[]{:S(2)}) async-start(bf16[4,2,8,1024]{3,2,1,0:T(8,128)(2,1)} %bitcast.16), calls=%async_computation.1 | async-start | bytes 262144 | tf_op jit(solution)/shard_map/all_to_all | solution.py:64
  101.2 0.9 fusion.53
  102.0 0.5 collective-permute-start.7
  102.5 1.4 %collective-permute-start.8 = (f32[8,8,4,2,16]{4,1,3,2,0:T(8,128)}, f32[8,8,4,2,16]{4,1,3,2,0:T(8,128)}, u32[]{:S(2)}, u32[]{:S(2)}) collective-permute-start(f32[8,8,4,2,16]{4,1,3,2,0:T(8,128)} %get-tuple-element.9), channel_id=1, source_target_pairs={{4,0},{8,4},{12,8},{0,12},{5,1},{9,5},{13,9},{1,13},{6,2},{10,6},{... | collective-permute-start | bytes 98312 | tf_op jit(solution)/shard_map/ppermute | solution.py:17
  104.0 0.6 collective-permute-start.9
  104.6 2.9 %copy.74 = f32[8,8,4,16,2]{4,1,3,2,0:T(8,128)} copy(f32[8,8,4,16,2]{3,1,4,2,0:T(8,128)S(1)} %collective-permute-done.10) | data formatting | bytes 65536 | tf_op jit(solution)/shard_map/ppermute | solution.py:17
  107.5 3.9 %copy.76 = f32[8,8,4,16,2]{4,1,3,2,0:T(8,128)} copy(f32[8,8,4,16,2]{3,1,4,2,0:T(8,128)} %collective-permute-done.11) | data formatting | bytes 65536 | tf_op jit(solution)/shard_map/ppermute | solution.py:16
  111.4 0.1 copy.92
  111.4 0.3 convolution_convert_fusion
  111.8 0.2 reshape.172
  112.0 5.6 %collective-permute-done.9 = f32[8,8,4,2,16]{4,1,3,2,0:T(8,128)} collective-permute-done((f32[8,8,4,2,16]{4,1,3,2,0:T(8,128)}, f32[8,8,4,2,16]{4,1,3,2,0:T(8,128)}, u32[]{:S(2)}, u32[]{:S(2)}) %collective-permute-start.9) | collective-permute-done | bytes 32800 | tf_op jit(solution)/shard_map/ppermute | solution.py:16
  117.7 17.4 %fusion.15 = f32[8,8,4,16,16]{4,1,3,2,0:T(8,128)S(1)} fusion(f32[8,8,4,16,16]{4,1,3,2,0:T(8,128)S(1)} %get-tuple-element.25, f32[8,8,4,2,16]{4,1,3,2,0:T(8,128)} %collective-permute-done.9, f32[8,8,4,2,16]{4,1,3,2,0:T(8,128)} %collective-permute-done.8, f32[2,8,4,16,16]{4,1,3,2,0:T(8,128)} %collective-permute-done.7, ...), kind=kOutput, calls=%fused_computation.27 | convolution fusion | flops 539033600 | bytes 9830400 | tf_op jit(solution)/shard_map/tmk,tlk->ml/dot_general | solution.py:71
  135.1 1.7 %copy.80 = f32[8,8,4,16,16]{4,3,2,1,0:T(8,128)} copy(f32[8,8,4,16,16]{4,1,3,2,0:T(8,128)S(1)} %fusion.15) | data formatting | bytes 524288 | tf_op jit(solution)/shard_map/sub | solution.py:73
  (37 shorter events, 0.1 us)
Async XLA Ops:
  2.8 1.7 %copy-start.1 = (f32[8,8,4,16,16]{4,1,3,2,0:T(8,128)}, f32[8,8,4,16,16]{4,1,3,2,0:T(8,128)S(1)}, u32[]{:S(2)}) copy-start(f32[8,8,4,16,16]{4,1,3,2,0:T(8,128)S(1)} %copy.66) | copy-start | bytes 786436
  2.8 5.4 %copy-start = (f32[8,8,4,16,16]{4,3,2,1,0:T(8,128)S(1)}, f32[8,8,4,16,16]{4,3,2,1,0:T(8,128)}, u32[]{:S(2)}) copy-start(f32[8,8,4,16,16]{4,3,2,1,0:T(8,128)} %param.8) | copy-start | bytes 786436
  3.9 4.6 %copy-start.9 = (s32[1,1,1,4,2]{3,4,2,1,0:T(2,128)S(1)}, s32[1,1,1,4,2]{3,4,2,1,0:T(2,128)}, u32[]{:S(2)}) copy-start(s32[1,1,1,4,2]{3,4,2,1,0:T(2,128)} %param.12) | copy-start | bytes 100
  3.9 40.9 %collective-permute-start.1 = (f32[2,8,4,16,16]{4,1,3,2,0:T(8,128)}, f32[2,8,4,16,16]{4,1,3,2,0:T(8,128)}, u32[]{:S(2)}, u32[]{:S(2)}) collective-permute-start(f32[2,8,4,16,16]{4,1,3,2,0:T(8,128)} %get-tuple-element.12), channel_id=1, source_target_pairs={{0,16},{16,0},{1,17},{17,1},{2,18},{18,2},{3,19},{19,3},{4,20},{20... | collective-permute-start | bytes 196616 | tf_op jit(solution)/shard_map/ppermute | solution.py:16
  5.3 38.5 %collective-permute-start.3 = (f32[8,8,4,2,16]{4,1,3,2,0:T(8,128)}, f32[8,8,4,2,16]{4,1,3,2,0:T(8,128)}, u32[]{:S(2)}, u32[]{:S(2)}) collective-permute-start(f32[8,8,4,2,16]{4,1,3,2,0:T(8,128)} %get-tuple-element.18), channel_id=1, source_target_pairs={{0,4},{4,8},{8,12},{12,0},{1,5},{5,9},{9,13},{13,1},{2,6},{6,10},{... | collective-permute-start | bytes 98312 | tf_op jit(solution)/shard_map/ppermute | solution.py:16
  8.2 42.4 %collective-permute-start = (f32[2,8,4,16,16]{4,1,3,2,0:T(8,128)}, f32[2,8,4,16,16]{4,1,3,2,0:T(8,128)}, u32[]{:S(2)}, u32[]{:S(2)}) collective-permute-start(f32[2,8,4,16,16]{4,1,3,2,0:T(8,128)} %get-tuple-element.11), channel_id=1, source_target_pairs={{16,0},{0,16},{17,1},{1,17},{18,2},{2,18},{19,3},{3,19},{20,4},{4,... | collective-permute-start | bytes 196616 | tf_op jit(solution)/shard_map/ppermute | solution.py:17
  11.6 42.4 %all-to-all-start = ((bf16[4,2,8,1024]{3,2,1,0:T(8,128)(2,1)}), bf16[4,2,8,1024]{3,2,1,0:T(8,128)(2,1)S(1)}, u32[]{:S(2)}, u32[]{:S(2)}) async-start(bf16[4,2,8,1024]{3,2,1,0:T(8,128)(2,1)} %bitcast.7), calls=%async_computation | async-start | bytes 262144 | tf_op jit(solution)/shard_map/all_to_all | solution.py:64
  19.3 11.0 %copy-start.2 = (f32[8,3,4,16,16]{4,3,2,1,0:T(8,128)S(1)}, f32[8,3,4,16,16]{4,3,2,1,0:T(8,128)}, u32[]{:S(2)}) copy-start(f32[8,3,4,16,16]{4,3,2,1,0:T(8,128)} %param.9) | copy-start | bytes 294916
  23.2 7.9 %copy-start.10 = (s32[1,1,1,4,2]{3,4,2,1,0:T(2,128)S(1)}, s32[1,1,1,4,2]{3,4,2,1,0:T(2,128)}, u32[]{:S(2)}) copy-start(s32[1,1,1,4,2]{3,4,2,1,0:T(2,128)} %param.13) | copy-start | bytes 100
  23.2 8.1 %copy-start.11 = (s32[1,1,1,4,2]{3,4,2,1,0:T(2,128)S(1)}, s32[1,1,1,4,2]{3,4,2,1,0:T(2,128)}, u32[]{:S(2)}) copy-start(s32[1,1,1,4,2]{3,4,2,1,0:T(2,128)} %param.14) | copy-start | bytes 100
  23.2 8.3 %copy-start.12 = (s32[1,1,1,4]{3,2,1,0:T(1,128)S(1)}, s32[1,1,1,4]{3,2,1,0:T(1,128)}, u32[]{:S(2)}) copy-start(s32[1,1,1,4]{3,2,1,0:T(1,128)} %param.15) | copy-start | bytes 52
  23.2 10.9 %collective-permute-start.4 = (f32[8,8,4,16,2]{3,1,4,2,0:T(8,128)}, f32[8,8,4,16,2]{3,1,4,2,0:T(8,128)S(1)}, u32[]{:S(2)}, u32[]{:S(2)}) collective-permute-start(f32[8,8,4,16,2]{3,1,4,2,0:T(8,128)} %copy.89), channel_id=1, source_target_pairs={{1,0},{2,1},{3,2},{0,3},{5,4},{6,5},{7,6},{4,7},{9,8},{10,9},{11,1... | collective-permute-start | bytes 98312 | tf_op jit(solution)/shard_map/ppermute | solution.py:17
  30.2 9.8 %collective-permute-start.5 = (f32[8,8,4,16,2]{3,1,4,2,0:T(8,128)S(1)}, f32[8,8,4,16,2]{3,1,4,2,0:T(8,128)}, u32[]{:S(2)}, u32[]{:S(2)}) collective-permute-start(f32[8,8,4,16,2]{3,1,4,2,0:T(8,128)S(1)} %copy.90), channel_id=1, source_target_pairs={{0,1},{1,2},{2,3},{3,0},{4,5},{5,6},{6,7},{7,4},{8,9},{9,10},{10,1... | collective-permute-start | bytes 98312 | tf_op jit(solution)/shard_map/ppermute | solution.py:16
  34.1 15.8 %collective-permute-start.2 = (f32[8,8,4,2,16]{4,1,3,2,0:T(8,128)}, f32[8,8,4,2,16]{4,1,3,2,0:T(8,128)S(1)}, u32[]{:S(2)}, u32[]{:S(2)}) collective-permute-start(f32[8,8,4,2,16]{4,1,3,2,0:T(8,128)} %get-tuple-element.17), channel_id=1, source_target_pairs={{4,0},{8,4},{12,8},{0,12},{5,1},{9,5},{13,9},{1,13},{6,2},{10,6},{... | collective-permute-start | bytes 98312 | tf_op jit(solution)/shard_map/ppermute | solution.py:17
  49.9 1.6 %copy-start.7 = (f32[10,8,4,16,16]{4,1,3,2,0:T(8,128)}, f32[10,8,4,16,16]{4,1,3,2,0:T(8,128)S(1)}, u32[]{:S(2)}) copy-start(f32[10,8,4,16,16]{4,1,3,2,0:T(8,128)S(1)} %get-tuple-element.14) | copy-start | bytes 983044
  49.9 2.3 %copy-start.8 = (f32[8,8,4,18,16]{4,1,3,2,0:T(8,128)}, f32[8,8,4,18,16]{4,1,3,2,0:T(8,128)S(1)}, u32[]{:S(2)}) copy-start(f32[8,8,4,18,16]{4,1,3,2,0:T(8,128)S(1)} %get-tuple-element.16) | copy-start | bytes 884740
  49.9 4.9 %copy-start.3 = (f32[8,4,16,16]{3,2,1,0:T(8,128)S(1)}, f32[8,4,16,16]{3,2,1,0:T(8,128)}, u32[]{:S(2)}) copy-start(f32[8,4,16,16]{3,2,1,0:T(8,128)} %get-tuple-element.21) | copy-start | bytes 98308
  49.9 4.9 %copy-start.5 = (f32[8,4,16,16]{3,2,1,0:T(8,128)S(1)}, f32[8,4,16,16]{3,2,1,0:T(8,128)}, u32[]{:S(2)}) copy-start(f32[8,4,16,16]{3,2,1,0:T(8,128)} %get-tuple-element.22) | copy-start | bytes 98308
  49.9 4.9 %copy-start.6 = (f32[8,4,16,16]{3,2,1,0:T(8,128)S(1)}, f32[8,4,16,16]{3,2,1,0:T(8,128)}, u32[]{:S(2)}) copy-start(f32[8,4,16,16]{3,2,1,0:T(8,128)} %get-tuple-element.23) | copy-start | bytes 98308
  84.8 19.2 %collective-permute-start.10 = (f32[8,8,4,16,2]{3,1,4,2,0:T(8,128)}, f32[8,8,4,16,2]{3,1,4,2,0:T(8,128)S(1)}, u32[]{:S(2)}, u32[]{:S(2)}) collective-permute-start(f32[8,8,4,16,2]{3,1,4,2,0:T(8,128)} %copy.73), channel_id=1, source_target_pairs={{1,0},{2,1},{3,2},{0,3},{5,4},{6,5},{7,6},{4,7},{9,8},{10,9},{11,1... | collective-permute-start | bytes 98312 | tf_op jit(solution)/shard_map/ppermute | solution.py:17
  91.6 15.9 %collective-permute-start.11 = (f32[8,8,4,16,2]{3,1,4,2,0:T(8,128)}, f32[8,8,4,16,2]{3,1,4,2,0:T(8,128)}, u32[]{:S(2)}, u32[]{:S(2)}) collective-permute-start(f32[8,8,4,16,2]{3,1,4,2,0:T(8,128)} %copy.75), channel_id=1, source_target_pairs={{0,1},{1,2},{2,3},{3,0},{4,5},{5,6},{6,7},{7,4},{8,9},{9,10},{10,1... | collective-permute-start | bytes 98312 | tf_op jit(solution)/shard_map/ppermute | solution.py:16
  96.1 15.3 %all-to-all-start.1 = ((bf16[4,2,8,1024]{3,2,1,0:T(8,128)(2,1)}), bf16[4,2,8,1024]{3,2,1,0:T(8,128)(2,1)S(1)}, u32[]{:S(2)}, u32[]{:S(2)}) async-start(bf16[4,2,8,1024]{3,2,1,0:T(8,128)(2,1)} %bitcast.16), calls=%async_computation.1 | async-start | bytes 262144 | tf_op jit(solution)/shard_map/all_to_all | solution.py:64
  102.0 15.6 %collective-permute-start.6 = (f32[2,8,4,16,16]{4,1,3,2,0:T(8,128)}, f32[2,8,4,16,16]{4,1,3,2,0:T(8,128)}, u32[]{:S(2)}, u32[]{:S(2)}) collective-permute-start(f32[2,8,4,16,16]{4,1,3,2,0:T(8,128)} %get-tuple-element.7), channel_id=1, source_target_pairs={{16,0},{0,16},{17,1},{1,17},{18,2},{2,18},{19,3},{3,19},{20,4},{4,... | collective-permute-start | bytes 196616 | tf_op jit(solution)/shard_map/ppermute | solution.py:17
  102.0 15.6 %collective-permute-start.7 = (f32[2,8,4,16,16]{4,1,3,2,0:T(8,128)}, f32[2,8,4,16,16]{4,1,3,2,0:T(8,128)}, u32[]{:S(2)}, u32[]{:S(2)}) collective-permute-start(f32[2,8,4,16,16]{4,1,3,2,0:T(8,128)} %get-tuple-element.8), channel_id=1, source_target_pairs={{0,16},{16,0},{1,17},{17,1},{2,18},{18,2},{3,19},{19,3},{4,20},{20... | collective-permute-start | bytes 196616 | tf_op jit(solution)/shard_map/ppermute | solution.py:16
  102.5 9.5 %collective-permute-start.8 = (f32[8,8,4,2,16]{4,1,3,2,0:T(8,128)}, f32[8,8,4,2,16]{4,1,3,2,0:T(8,128)}, u32[]{:S(2)}, u32[]{:S(2)}) collective-permute-start(f32[8,8,4,2,16]{4,1,3,2,0:T(8,128)} %get-tuple-element.9), channel_id=1, source_target_pairs={{4,0},{8,4},{12,8},{0,12},{5,1},{9,5},{13,9},{1,13},{6,2},{10,6},{... | collective-permute-start | bytes 98312 | tf_op jit(solution)/shard_map/ppermute | solution.py:17
  104.0 13.7 %collective-permute-start.9 = (f32[8,8,4,2,16]{4,1,3,2,0:T(8,128)}, f32[8,8,4,2,16]{4,1,3,2,0:T(8,128)}, u32[]{:S(2)}, u32[]{:S(2)}) collective-permute-start(f32[8,8,4,2,16]{4,1,3,2,0:T(8,128)} %get-tuple-element.10), channel_id=1, source_target_pairs={{0,4},{4,8},{8,12},{12,0},{1,5},{5,9},{9,13},{13,1},{2,6},{6,10},{... | collective-permute-start | bytes 98312 | tf_op jit(solution)/shard_map/ppermute | solution.py:16
  107.5 10.2 %copy-start.4 = (f32[8,4,16,16]{3,2,1,0:T(8,128)S(1)}, f32[8,4,16,16]{3,2,1,0:T(8,128)}, u32[]{:S(2)}) copy-start(f32[8,4,16,16]{3,2,1,0:T(8,128)} %get-tuple-element.21) | copy-start | bytes 98308
where the time goes:
time: 137 us
  local copies, waits for them, and re-layouts  61.1 us (45%)
  matrix products  40.4 us (29%)
  starting transfers between devices  24.1 us (18%)
  waiting for transfers between devices  9.56 us (7%)
  other arithmetic  1.43 us (1%)
    dot_general x2, matrix products, per_device(): jnp.einsum('tmk,tlk->ml', grouped, tiles, preferred_element_type=jnp.floa...  39.7 us
    unnamed x35, local copies, waits for them, and re-layouts  17.8 us
    slice x7, local copies, waits for them, and re-layouts, extended(): leading = lax.slice_in_dim(x, 0, width, axis=dim)  13.2 us
    all_to_all x2, starting transfers between devices, per_device(): lax.all_to_all(outgoing, 'kz', split_axis=0, concat_axis=0, tiled=True)  9.96 us
    ppermute x6, starting transfers between devices, extended(): after = lax.ppermute(leading, axis, down)  9.62 us
    ppermute x2, local copies, waits for them, and re-layouts, extended(): before = lax.ppermute(last, axis, up)  7.69 us
    ppermute x6, waiting for transfers between devices, extended(): before = lax.ppermute(last, axis, up)  7.19 us
    ppermute x2, local copies, waits for them, and re-layouts, extended(): after = lax.ppermute(leading, axis, down)  5.81 us
  transfers between devices with their start and end apart: 14, of which 3 were waited for; matrix products, arithmetic and copies ran while one was open for 35% of the time, Pallas kernels for 0%

commit v1 on v0

v1 whole, which is shorter than its diff:
```python
import functools
import jax
import jax.numpy as jnp
from jax import lax
from jax.experimental import pallas as pl
from jax.experimental.pallas import tpu as pltpu
from jax.sharding import PartitionSpec as P

ITERS = 2
MESH = pl.DeviceIdType.MESH
LANES = 128


def roll(v, by):
    by = by % LANES
    return v if by == 0 else pltpu.roll(v, by, axis=1)


def main_kernel(sizes, pop, force, rate, tiles, send_planes, recv_target, recv_tile, recv_count, out,
                pop_in, force_in, rate_in, tiles_in, ext, mid, field, base, y_out, y_in, z_out, z_in,
                p_out, p_in, in_sem, tile_sem, x_send, x_recv, y_send, y_recv, z_send, z_recv, p_send, p_recv):
    n_x, n_y, n_z, wx, drives, bands, wy, wz, cap, n_tiles = sizes
    rows = bands * wy
    length = rows * wz
    pieces = length // LANES
    per = LANES // wz
    halves = wy // per
    mx, my, mz = lax.axis_index("kx"), lax.axis_index("ky"), lax.axis_index("kz")

    def around(me, size, by):
        return lax.rem(me + (by % size), size)

    barrier = pltpu.get_barrier_semaphore()
    friends = []
    for name, me, size, offsets in (("kx", mx, n_x, {1, n_x - 1}), ("ky", my, n_y, {1, n_y - 1}), ("kz", mz, n_z, set(range(1, n_z)))):
        for by in sorted(offsets):
            friends.append({name: around(me, size, by)})
    for friend in friends:
        pl.semaphore_signal(barrier, inc=1, device_id=friend, device_id_type=MESH)

    loads = [pltpu.make_async_copy(a, b, in_sem.at[i]) for i, (a, b) in enumerate(((pop, pop_in), (force, force_in), (rate, rate_in)))]
    for load in loads:
        load.start()
    tile_loads = [pltpu.make_async_copy(tiles.at[t], tiles_in.at[t], tile_sem.at[t]) for t in range(n_tiles)]
    for load in tile_loads:
        load.start()

    lane = lax.broadcasted_iota(jnp.int32, (8, LANES), 1)
    z_of = lax.rem(lane, wz)

    loads[0].wait()

    def lay_pop(x, carry):
        for v in range(pieces):
            piece = jnp.concatenate(
                [pop_in[pl.ds(x * drives * rows + v * per + i, drives, stride=rows), :] for i in range(per)], axis=1)
            ext[0, x + 2, :, v * LANES:(v + 1) * LANES] = piece
            mid[x, :, v * LANES:(v + 1) * LANES] = piece
        return carry

    lax.fori_loop(0, wx, lay_pop, 0)
    pl.semaphore_wait(barrier, len(friends))

    sel = None
    in_flight = []
    for it in range(ITERS):
        cur = ext.at[it]
        waits_p = []
        for k in range(n_z - 1, -1, -1):
            peer = around(mz, n_z, k)
            blocks = jnp.concatenate(
                [mid[send_planes[0, 0, 0, c, peer]] for c in range(cap)], axis=0).astype(jnp.bfloat16)
            if k == 0:
                p_in[it, 0:cap * drives, :] = blocks
            else:
                p_out[it, k * cap * drives:(k + 1) * cap * drives, :] = blocks
                part = pl.ds(k * cap * drives, cap * drives)
                copy = pltpu.make_async_remote_copy(
                    p_out.at[it, part], p_in.at[it, part], p_send.at[it, k], p_recv.at[it, k],
                    device_id={"kz": peer}, device_id_type=MESH)
                copy.start()
                waits_p.append(copy)
        waits_h = [
            pltpu.make_async_remote_copy(
                cur.at[wx:wx + 2], cur.at[0:2], x_send.at[it, 0], x_recv.at[it, 0],
                device_id={"kx": around(mx, n_x, 1)}, device_id_type=MESH),
            pltpu.make_async_remote_copy(
                cur.at[2:4], cur.at[wx + 2:wx + 4], x_send.at[it, 1], x_recv.at[it, 1],
                device_id={"kx": around(mx, n_x, -1)}, device_id_type=MESH)]
        for copy in waits_h:
            copy.start()

        def pack(x, carry):
            part = [cur[x + 2, :, v * LANES:(v + 1) * LANES] for v in range(pieces)]
            up_z = jnp.zeros((drives, LANES), jnp.float32)
            down_z = up_z
            for v in range(pieces):
                c = part[v]
                last = jnp.where(z_of == wz - 2, c - 8.0 * roll(c, -1), c)
                first = jnp.where(z_of == 0, -c, 8.0 * roll(c, 1) - c)
                here = lax.div(z_of, 2) == v
                up_z = jnp.where(here, roll(last, 2 * v - (wz - 2)), up_z)
                down_z = jnp.where(here, roll(first, 2 * v), down_z)
            z_out[it, 0, x] = up_z
            z_out[it, 1, x] = down_z
            up_y = jnp.zeros((drives, LANES), jnp.float32)
            down_y = up_y
            width = 2 * wz
            for b in range(bands):
                here = lax.div(lane, width) == b
                up_y = jnp.where(here, roll(part[b * halves + halves - 1], width * b - (LANES - width)), up_y)
                down_y = jnp.where(here, roll(part[b * halves], width * b), down_y)
            y_out[it, 0, x] = up_y
            y_out[it, 1, x] = down_y
            return carry

        lax.fori_loop(0, wx, pack, 0)
        for name, me, size, o, i, ss, rs in (("kz", mz, n_z, z_out, z_in, z_send, z_recv), ("ky", my, n_y, y_out, y_in, y_send, y_recv)):
            for way in range(2):
                copy = pltpu.make_async_remote_copy(
                    o.at[it, way], i.at[it, way], ss.at[it, way], rs.at[it, way],
                    device_id={name: around(me, size, 1 if way == 0 else -1)}, device_id_type=MESH)
                copy.start()
                waits_h.append(copy)

        if it == 0:
            loads[1].wait()
            loads[2].wait()
            for v in range(pieces):
                at = slice(v * LANES, (v + 1) * LANES)
                for a in range(4):
                    source, first, stride = (force_in, a * rows, 3 * rows) if a < 3 else (rate_in, 0, rows)
                    piece = jnp.concatenate(
                        [source[pl.ds(first + v * per + i, wx, stride=stride), :] for i in range(per)], axis=1)
                    if a < 3:
                        piece = piece * (1.0 / 12.0)
                    for x in range(wx):
                        field[a, x, :, at] = jnp.broadcast_to(piece[x:x + 1], (drives, LANES))
            slots = n_z * cap
            col = lax.broadcasted_iota(jnp.int32, (8, slots * drives), 1)
            pair = jnp.full((8, slots * drives), -1, jnp.int32)
            for k in range(n_z):
                source = around(mz, n_z, -k)
                count = recv_count[0, 0, 0, source]
                for c in range(cap):
                    code = jnp.where(c < count, recv_tile[0, 0, 0, c, source] * wx + recv_target[0, 0, 0, c, source], -1)
                    pair = jnp.where(lax.div(col, drives) == k * cap + c, code, pair)
            row = lax.broadcasted_iota(jnp.int32, (n_tiles * wx * drives, slots * drives), 0)
            col = lax.broadcasted_iota(jnp.int32, (n_tiles * wx * drives, slots * drives), 1)
            hit = (lax.div(row, drives) == pair[0:1]) & (lax.rem(row, drives) == lax.rem(col, drives))
            sel = jnp.where(hit, 1.0, 0.0).astype(jnp.bfloat16)

        for copy in waits_h:
            copy.wait_recv()

        def step(x, carry):
            zp, zn = z_in[it, 0, x], z_in[it, 1, x]
            yp, yn = y_in[it, 0, x], y_in[it, 1, x]
            width = 2 * wz
            part = [cur[x + 2, :, v * LANES:(v + 1) * LANES] for v in range(pieces)]
            for v in range(pieces):
                at = slice(v * LANES, (v + 1) * LANES)
                b, h = divmod(v, halves)
                c = part[v]
                dx = 8.0 * (cur[x + 3, :, at] - cur[x + 1, :, at]) - (cur[x + 4, :, at] - cur[x, :, at])
                after = part[v + 1] if h < halves - 1 else roll(yn, -width * b)
                before = part[v - 1] if h > 0 else roll(yp, LANES - width - width * b)
                y1 = roll(jnp.where(lane < wz, after, c), -wz)
                y2 = roll(jnp.where(lane < 2 * wz, after, c), -2 * wz)
                w1 = roll(jnp.where(lane >= LANES - wz, before, c), wz)
                w2 = roll(jnp.where(lane >= LANES - 2 * wz, before, c), 2 * wz)
                dy = 8.0 * (y1 - w1) - (y2 - w2)
                a1 = jnp.where(z_of < wz - 1, roll(c, -1), 0.0)
                b1 = jnp.where(z_of >= 1, roll(c, 1), 0.0)
                a2 = jnp.where(z_of < wz - 2, roll(c, -2), 0.0)
                b2 = jnp.where(z_of >= 2, roll(c, 2), 0.0)
                edge = jnp.where(z_of < 2, roll(zp, -2 * v), jnp.where(z_of >= wz - 2, roll(zn, wz - 2 - 2 * v), 0.0))
                dz = 8.0 * (a1 - b1) - (a2 - b2) + edge
                fx, fy, fz, r = (field[a, x, :, at] for a in range(4))
                base[pl.ds(pl.multiple_of(x * drives, drives), drives), at] = c - (fx * dx + fy * dy + fz * dz) - r * c
            return carry

        lax.fori_loop(0, wx, step, 0)

        for copy in waits_p:
            copy.wait_recv()
        grouped = jnp.dot(sel, p_in[it], preferred_element_type=jnp.float32).astype(jnp.bfloat16)
        m = wx * drives
        total = base[...]
        for t in range(n_tiles):
            if it == 0:
                tile_loads[t].wait()
            total = total + lax.dot_general(
                grouped[t * m:(t + 1) * m], tiles_in[t], (((1,), (1,)), ((), ())), preferred_element_type=jnp.float32)
        total = total.reshape(wx, drives, length)
        if it == ITERS - 1:
            out[...] = total
        else:
            ext[it + 1, 2:wx + 2] = total
            mid[...] = total
        in_flight += waits_p + waits_h
    for copy in in_flight:
        copy.wait_send()


def spread_kernel(sizes, dense, out):
    wx, drives, rows, wz = sizes
    per = LANES // wz
    pieces = rows // per

    def lay(x, carry):
        for v in range(pieces):
            piece = dense[x, :, v * LANES:(v + 1) * LANES]
            for i in range(per):
                out[pl.ds(x * drives * rows + v * per + i, drives, stride=rows), :] = roll(piece, -i * wz)[:, :wz]
        return carry

    lax.fori_loop(0, wx, lay, 0)


def per_device(mesh_shape, populations, force, rate, tiles, send_planes, recv_target, recv_tile, recv_count):
    wx, drives, bands, wy, wz = populations.shape
    cap = send_planes.shape[-1]
    n_tiles, length, _ = tiles.shape
    n_x, n_y, n_z = mesh_shape
    rows = bands * wy
    sizes = (n_x, n_y, n_z, wx, drives, bands, wy, wz, cap, n_tiles)
    vmem = pl.BlockSpec(memory_space=pltpu.VMEM)
    smem = pl.BlockSpec(memory_space=pltpu.SMEM)
    anywhere = pl.BlockSpec(memory_space=pl.ANY)
    f32, b16 = jnp.float32, jnp.bfloat16
    dma = pltpu.SemaphoreType.DMA
    dense = pl.pallas_call(
        functools.partial(main_kernel, sizes),
        out_shape=jax.ShapeDtypeStruct((wx, drives, length), f32),
        in_specs=[anywhere] * 4 + [smem] * 4,
        out_specs=vmem,
        scratch_shapes=[
            pltpu.VMEM((wx * drives * rows, wz), f32),
            pltpu.VMEM((wx * 3 * rows, wz), f32),
            pltpu.VMEM((wx * rows, wz), f32),
            pltpu.VMEM(tiles.shape, b16),
            pltpu.VMEM((ITERS, wx + 4, drives, length), f32),
            pltpu.VMEM((wx, drives, length), f32),
            pltpu.VMEM((4, wx, drives, length), f32),
            pltpu.VMEM((wx * drives, length), f32),
            pltpu.VMEM((ITERS, 2, wx, drives, LANES), f32),
            pltpu.VMEM((ITERS, 2, wx, drives, LANES), f32),
            pltpu.VMEM((ITERS, 2, wx, drives, LANES), f32),
            pltpu.VMEM((ITERS, 2, wx, drives, LANES), f32),
            pltpu.VMEM((ITERS, n_z * cap * drives, length), b16),
            pltpu.VMEM((ITERS, n_z * cap * drives, length), b16),
            dma((3,)), dma((n_tiles,)),
            dma((ITERS, 2)), dma((ITERS, 2)), dma((ITERS, 2)), dma((ITERS, 2)), dma((ITERS, 2)), dma((ITERS, 2)),
            dma((ITERS, n_z)), dma((ITERS, n_z)),
        ],
        compiler_params=pltpu.CompilerParams(collective_id=0, has_side_effects=True, vmem_limit_bytes=48 * 2**20),
        name="steps",
    )(
        populations.reshape(wx * drives * rows, wz),
        force.reshape(wx * 3 * rows, wz),
        rate.reshape(wx * rows, wz),
        tiles,
        jnp.swapaxes(send_planes, -1, -2),
        jnp.swapaxes(recv_target, -1, -2),
        jnp.swapaxes(recv_tile, -1, -2),
        recv_count,
    )
    spread = pl.pallas_call(
        functools.partial(spread_kernel, (wx, drives, rows, wz)),
        out_shape=jax.ShapeDtypeStruct((wx * drives * rows, wz), f32),
        in_specs=[vmem],
        out_specs=vmem,
        compiler_params=pltpu.CompilerParams(vmem_limit_bytes=16 * 2**20),
        name="spread",
    )(dense)
    return spread.reshape(populations.shape)


def solution(mesh):
    placed = (
        P("kx", None, None, "ky", "kz"),
        P("kx", None, None, "ky", "kz"),
        P("kx", None, "ky", "kz"),
        P(),
        P("kx", "ky", "kz", None, None),
        P("kx", "ky", "kz", None, None),
        P("kx", "ky", "kz", None, None),
        P("kx", "ky", "kz", None),
    )
    sizes = tuple(mesh.shape[a] for a in ("kx", "ky", "kz"))
    return jax.shard_map(
        functools.partial(per_device, sizes),
        mesh=mesh,
        in_specs=placed,
        out_specs=P("kx", None, None, "ky", "kz"),
        check_vma=False,
    )
```

time: 137 us -> 35.5 us (0.26)
  local copies, waits for them, and re-layouts: 61.1 us -> 6.36 us
  matrix products: 40.4 us -> 0 us
  Pallas kernels: 0 us -> 28.8 us
  starting transfers between devices: 24.1 us -> 0 us
  waiting for transfers between devices: 9.56 us -> 0 us
  other arithmetic: 1.43 us -> 0 us
    dot_general x4 -> x0, matrix products: 40.4 us -> none  [the longest x2 39.7 us: per_device(): jnp.einsum('tmk,tlk->ml', grouped, tiles, preferred_element_type=jnp.floa...]
    pallas_call x0 -> x2, Pallas kernels: none -> 28.8 us  [the longest x1 26 us: per_device(): pl.pallas_call(functools.partial(main_kernel, sizes), out_shape=jax.Shape...]
    slice x8 -> x0, local copies, waits for them, and re-layouts: 17.1 us -> none  [the longest x7 13.2 us: extended(): leading = lax.slice_in_dim(x, 0, width, axis=dim)]
    ppermute x12 -> x0, starting transfers between devices: 14.2 us -> none  [the longest x6 9.62 us: extended(): after = lax.ppermute(leading, axis, down)]
    ppermute x4 -> x0, local copies, waits for them, and re-layouts: 13.5 us -> none  [the longest x2 7.69 us: extended(): before = lax.ppermute(last, axis, up)]
    unnamed x35 -> x14, local copies, waits for them, and re-layouts: 17.8 us -> 6.36 us
    all_to_all x2 -> x0, starting transfers between devices: 9.96 us -> none  [per_device(): lax.all_to_all(outgoing, 'kz', split_axis=0, concat_axis=0, tiled=True)]
    ppermute x12 -> x0, waiting for transfers between devices: 9.55 us -> none  [the longest x6 7.19 us: extended(): before = lax.ppermute(last, axis, up)]
  transfers between devices with their start and end apart: 14 -> 0, of which waited for: 3 -> 0; matrix products, arithmetic and copies ran while one was open for 35% -> 0% of each run, Pallas kernels for 0% -> 0%
where the time goes in v1:
time: 35.5 us; the launch traced here: 35.2 us
  Pallas kernels  28.8 us (81%)
  local copies, waits for them, and re-layouts  6.36 us (18%)
    pallas_call x1, Pallas kernels, per_device(): pl.pallas_call(functools.partial(main_kernel, sizes), out_shape=jax.Shape...  26 us
    unnamed x14, local copies, waits for them, and re-layouts  6.36 us
    pallas_call x1, Pallas kernels, per_device(): pl.pallas_call(functools.partial(spread_kernel, (wx, drives, rows, wz)),...  2.84 us

profile of v1, /device:TPU:0, one launch (start us, length us, event | category | flops | bytes accessed | tf_op | source)
XLA Modules:
  0.0 35.2 jit_solution(5349975881868516777)
XLA Ops:
  0.0 0.0 copy-start
  0.0 1.6 %copy-done = f32[8,8,4,16,16]{4,3,2,1,0:T(8,128)S(1)} copy-done((f32[8,8,4,16,16]{4,3,2,1,0:T(8,128)S(1)}, f32[8,8,4,16,16]{4,3,2,1,0:T(8,128)}, u32[]{:S(2)}) %copy-start) | copy-done | bytes 262168
  1.6 0.0 copy-start.1
  1.6 1.1 %copy-done.1 = f32[8,3,4,16,16]{4,3,2,1,0:T(8,128)S(1)} copy-done((f32[8,3,4,16,16]{4,3,2,1,0:T(8,128)S(1)}, f32[8,3,4,16,16]{4,3,2,1,0:T(8,128)}, u32[]{:S(2)}) %copy-start.1) | copy-done | bytes 98328
  2.7 0.0 copy-start.2
  2.7 0.9 %copy-done.2 = f32[8,4,16,16]{3,2,1,0:T(8,128)S(1)} copy-done((f32[8,4,16,16]{3,2,1,0:T(8,128)S(1)}, f32[8,4,16,16]{3,2,1,0:T(8,128)}, u32[]{:S(2)}) %copy-start.2) | copy-done | bytes 32792
  3.7 0.0 copy-start.3
  3.7 0.7 %copy-done.3 = s32[1,1,1,4,2]{3,4,2,1,0:T(2,128)S(1)} copy-done((s32[1,1,1,4,2]{3,4,2,1,0:T(2,128)S(1)}, s32[1,1,1,4,2]{3,4,2,1,0:T(2,128)}, u32[]{:S(2)}) %copy-start.3) | copy-done | bytes 56
  4.4 0.0 copy-start.4
  4.4 0.7 %copy-done.4 = s32[1,1,1,4,2]{3,4,2,1,0:T(2,128)S(1)} copy-done((s32[1,1,1,4,2]{3,4,2,1,0:T(2,128)S(1)}, s32[1,1,1,4,2]{3,4,2,1,0:T(2,128)}, u32[]{:S(2)}) %copy-start.4) | copy-done | bytes 56
  5.0 0.0 copy-start.5
  5.0 0.7 %copy-done.5 = s32[1,1,1,4,2]{3,4,2,1,0:T(2,128)S(1)} copy-done((s32[1,1,1,4,2]{3,4,2,1,0:T(2,128)S(1)}, s32[1,1,1,4,2]{3,4,2,1,0:T(2,128)}, u32[]{:S(2)}) %copy-start.5) | copy-done | bytes 56
  5.7 0.0 copy-start.6
  5.7 0.7 %copy-done.6 = s32[1,1,1,4]{3,2,1,0:T(1,128)S(1)} copy-done((s32[1,1,1,4]{3,2,1,0:T(1,128)S(1)}, s32[1,1,1,4]{3,2,1,0:T(1,128)}, u32[]{:S(2)}) %copy-start.6) | copy-done | bytes 40
  6.4 26.0 %steps.1.dense = f32[8,8,1024]{2,1,0:T(8,128)S(1)} custom-call(f32[4096,16]{1,0:T(8,128)S(1)} %bitcast.7, f32[1536,16]{1,0:T(8,128)S(1)} %bitcast.8, f32[512,16]{1,0:T(8,128)S(1)} %bitcast.9, bf16[4,1024,1024]{2,1,0:T(8,128)(2,1)} %tiles.1, s32[1,1,1,2,4]{4,3,2,1,0:T(2,128)S(1)} %bitcast.10, s32[1,1,1,2,4]{4,3,2,1,0:T(2,128)S(1)} %bitcast.11, ...), custom_call_target="tpu_custom_call" | custom-call | tf_op jit(solution)/shard_map/steps/pallas_call | solution.py:233
  32.4 2.8 %spread.1 = f32[4096,16]{1,0:T(8,128)} custom-call(f32[8,8,1024]{2,1,0:T(8,128)S(1)} %steps.1.dense), custom_call_target="tpu_custom_call" | custom-call | tf_op jit(solution)/shard_map/spread/pallas_call | solution.py:269
Async XLA Ops:
  0.0 1.6 %copy-start = (f32[8,8,4,16,16]{4,3,2,1,0:T(8,128)S(1)}, f32[8,8,4,16,16]{4,3,2,1,0:T(8,128)}, u32[]{:S(2)}) copy-start(f32[8,8,4,16,16]{4,3,2,1,0:T(8,128)} %param.8) | copy-start | bytes 786436
  1.6 1.1 %copy-start.1 = (f32[8,3,4,16,16]{4,3,2,1,0:T(8,128)S(1)}, f32[8,3,4,16,16]{4,3,2,1,0:T(8,128)}, u32[]{:S(2)}) copy-start(f32[8,3,4,16,16]{4,3,2,1,0:T(8,128)} %param.9) | copy-start | bytes 294916
  2.7 0.9 %copy-start.2 = (f32[8,4,16,16]{3,2,1,0:T(8,128)S(1)}, f32[8,4,16,16]{3,2,1,0:T(8,128)}, u32[]{:S(2)}) copy-start(f32[8,4,16,16]{3,2,1,0:T(8,128)} %param.10) | copy-start | bytes 98308
  3.7 0.7 %copy-start.3 = (s32[1,1,1,4,2]{3,4,2,1,0:T(2,128)S(1)}, s32[1,1,1,4,2]{3,4,2,1,0:T(2,128)}, u32[]{:S(2)}) copy-start(s32[1,1,1,4,2]{3,4,2,1,0:T(2,128)} %param.12) | copy-start | bytes 100
  4.4 0.7 %copy-start.4 = (s32[1,1,1,4,2]{3,4,2,1,0:T(2,128)S(1)}, s32[1,1,1,4,2]{3,4,2,1,0:T(2,128)}, u32[]{:S(2)}) copy-start(s32[1,1,1,4,2]{3,4,2,1,0:T(2,128)} %param.13) | copy-start | bytes 100
  5.0 0.7 %copy-start.5 = (s32[1,1,1,4,2]{3,4,2,1,0:T(2,128)S(1)}, s32[1,1,1,4,2]{3,4,2,1,0:T(2,128)}, u32[]{:S(2)}) copy-start(s32[1,1,1,4,2]{3,4,2,1,0:T(2,128)} %param.14) | copy-start | bytes 100
  5.7 0.7 %copy-start.6 = (s32[1,1,1,4]{3,2,1,0:T(1,128)S(1)}, s32[1,1,1,4]{3,2,1,0:T(1,128)}, u32[]{:S(2)}) copy-start(s32[1,1,1,4]{3,2,1,0:T(1,128)} %recv_count.1) | copy-start | bytes 52

commit v2 on v1

--- a/solution.py
+++ b/solution.py
@@ -16,9 +16,9 @@
     return v if by == 0 else pltpu.roll(v, by, axis=1)
 
 
-def main_kernel(sizes, pop, force, rate, tiles, send_planes, recv_target, recv_tile, recv_count, out,
-                pop_in, force_in, rate_in, tiles_in, ext, mid, field, base, y_out, y_in, z_out, z_in,
-                p_out, p_in, in_sem, tile_sem, x_send, x_recv, y_send, y_recv, z_send, z_recv, p_send, p_recv):
+def main_kernel(sizes, pop, force, rate, tiles, send_hbm, target_hbm, tile_hbm, count_hbm, out,
+                send_planes, recv_target, recv_tile, recv_count, pop_in, force_in, rate_in, tiles_in, ext, mid, field, base, y_out, y_in, z_out, z_in,
+                p_out, p_in, in_sem, pop_sem, tile_sem, x_send, x_recv, y_send, y_recv, z_send, z_recv, p_send, p_recv):
     n_x, n_y, n_z, wx, drives, bands, wy, wz, cap, n_tiles = sizes
     rows = bands * wy
     length = rows * wz
@@ -38,7 +38,13 @@
     for friend in friends:
         pl.semaphore_signal(barrier, inc=1, device_id=friend, device_id_type=MESH)
 
-    loads = [pltpu.make_async_copy(a, b, in_sem.at[i]) for i, (a, b) in enumerate(((pop, pop_in), (force, force_in), (rate, rate_in)))]
+    pop_rows = drives * rows
+    pop_loads = [pltpu.make_async_copy(pop.at[pl.ds(x * pop_rows, pop_rows)], pop_in.at[pl.ds(x * pop_rows, pop_rows)], pop_sem.at[x])
+                 for x in range(wx)]
+    for load in pop_loads:
+        load.start()
+    pairs = ((send_hbm, send_planes), (target_hbm, recv_target), (tile_hbm, recv_tile), (count_hbm, recv_count), (force, force_in), (rate, rate_in))
+    loads = [pltpu.make_async_copy(a, b, in_sem.at[i]) for i, (a, b) in enumerate(pairs)]
     for load in loads:
         load.start()
     tile_loads = [pltpu.make_async_copy(tiles.at[t], tiles_in.at[t], tile_sem.at[t]) for t in range(n_tiles)]
@@ -48,17 +54,14 @@
     lane = lax.broadcasted_iota(jnp.int32, (8, LANES), 1)
     z_of = lax.rem(lane, wz)
 
-    loads[0].wait()
-
-    def lay_pop(x, carry):
+    for x in range(wx):
+        pop_loads[x].wait()
         for v in range(pieces):
             piece = jnp.concatenate(
-                [pop_in[pl.ds(x * drives * rows + v * per + i, drives, stride=rows), :] for i in range(per)], axis=1)
+                [pop_in[pl.ds(x * pop_rows + v * per + i, drives, stride=rows), :] for i in range(per)], axis=1)
             ext[0, x + 2, :, v * LANES:(v + 1) * LANES] = piece
             mid[x, :, v * LANES:(v + 1) * LANES] = piece
-        return carry
-
-    lax.fori_loop(0, wx, lay_pop, 0)
+    loads[0].wait()
     pl.semaphore_wait(barrier, len(friends))
 
     sel = None
@@ -124,8 +127,8 @@
                 waits_h.append(copy)
 
         if it == 0:
-            loads[1].wait()
-            loads[2].wait()
+            for load in loads[1:]:
+                load.wait()
             for v in range(pieces):
                 at = slice(v * LANES, (v + 1) * LANES)
                 for a in range(4):
@@ -203,19 +206,25 @@
         copy.wait_send()
 
 
-def spread_kernel(sizes, dense, out):
+def spread_kernel(sizes, dense_hbm, out, dense, laid, in_sem, sem):
     wx, drives, rows, wz = sizes
     per = LANES // wz
     pieces = rows // per
-
-    def lay(x, carry):
+    loads = [pltpu.make_async_copy(dense_hbm.at[x], dense.at[x], in_sem.at[x]) for x in range(wx)]
+    for load in loads:
+        load.start()
+    copies = []
+    for x in range(wx):
+        loads[x].wait()
         for v in range(pieces):
             piece = dense[x, :, v * LANES:(v + 1) * LANES]
             for i in range(per):
-                out[pl.ds(x * drives * rows + v * per + i, drives, stride=rows), :] = roll(piece, -i * wz)[:, :wz]
-        return carry
-
-    lax.fori_loop(0, wx, lay, 0)
+                laid[pl.ds(x * drives * rows + v * per + i, drives, stride=rows), :] = roll(piece, -i * wz)[:, :wz]
+        part = pl.ds(x * drives * rows, drives * rows)
+        copies.append(pltpu.make_async_copy(laid.at[part], out.at[part], sem.at[x]))
+        copies[-1].start()
+    for copy in copies:
+        copy.wait()
 
 
 def per_device(mesh_shape, populations, force, rate, tiles, send_planes, recv_target, recv_tile, recv_count):
@@ -226,16 +235,19 @@
     rows = bands * wy
     sizes = (n_x, n_y, n_z, wx, drives, bands, wy, wz, cap, n_tiles)
     vmem = pl.BlockSpec(memory_space=pltpu.VMEM)
-    smem = pl.BlockSpec(memory_space=pltpu.SMEM)
-    anywhere = pl.BlockSpec(memory_space=pl.ANY)
+    hbm = pl.BlockSpec(memory_space=pltpu.HBM)
     f32, b16 = jnp.float32, jnp.bfloat16
     dma = pltpu.SemaphoreType.DMA
     dense = pl.pallas_call(
         functools.partial(main_kernel, sizes),
         out_shape=jax.ShapeDtypeStruct((wx, drives, length), f32),
-        in_specs=[anywhere] * 4 + [smem] * 4,
+        in_specs=[hbm] * 8,
         out_specs=vmem,
         scratch_shapes=[
+            pltpu.SMEM((1, 1, 1, cap, n_z), jnp.int32),
+            pltpu.SMEM((1, 1, 1, cap, n_z), jnp.int32),
+            pltpu.SMEM((1, 1, 1, cap, n_z), jnp.int32),
+            pltpu.SMEM((1, 1, 1, n_z), jnp.int32),
             pltpu.VMEM((wx * drives * rows, wz), f32),
             pltpu.VMEM((wx * 3 * rows, wz), f32),
             pltpu.VMEM((wx * rows, wz), f32),
@@ -250,11 +262,11 @@
             pltpu.VMEM((ITERS, 2, wx, drives, LANES), f32),
             pltpu.VMEM((ITERS, n_z * cap * drives, length), b16),
             pltpu.VMEM((ITERS, n_z * cap * drives, length), b16),
-            dma((3,)), dma((n_tiles,)),
+            dma((6,)), dma((wx,)), dma((n_tiles,)),
             dma((ITERS, 2)), dma((ITERS, 2)), dma((ITERS, 2)), dma((ITERS, 2)), dma((ITERS, 2)), dma((ITERS, 2)),
             dma((ITERS, n_z)), dma((ITERS, n_z)),
         ],
-        compiler_params=pltpu.CompilerParams(collective_id=0, has_side_effects=True, vmem_limit_bytes=48 * 2**20),
+        compiler_params=pltpu.CompilerParams(collective_id=0, has_side_effects=True, vmem_limit_bytes=60 * 2**20),
         name="steps",
     )(
         populations.reshape(wx * drives * rows, wz),
@@ -269,9 +281,10 @@
     spread = pl.pallas_call(
         functools.partial(spread_kernel, (wx, drives, rows, wz)),
         out_shape=jax.ShapeDtypeStruct((wx * drives * rows, wz), f32),
-        in_specs=[vmem],
-        out_specs=vmem,
-        compiler_params=pltpu.CompilerParams(vmem_limit_bytes=16 * 2**20),
+        in_specs=[hbm],
+        out_specs=hbm,
+        scratch_shapes=[pltpu.VMEM((wx, drives, length), f32), pltpu.VMEM((wx * drives * rows, wz), f32), dma((wx,)), dma((wx,))],
+        compiler_params=pltpu.CompilerParams(vmem_limit_bytes=60 * 2**20),
         name="spread",
     )(dense)
     return spread.reshape(populations.shape)

time: 35.5 us -> 31.5 us (0.89)
  local copies, waits for them, and re-layouts: 6.36 us -> 0 us
  Pallas kernels: 28.8 us -> 31.3 us
    unnamed x14 -> x0, local copies, waits for them, and re-layouts: 6.36 us -> none
    pallas_call x1, Pallas kernels: 26 us -> 28.1 us  [per_device(): pl.pallas_call(functools.partial(main_kernel, sizes), out_shape=jax.Shape...]
where the time goes in v2:
time: 31.5 us; the launch traced here: 31.3 us
  Pallas kernels  31.3 us (99%)
    pallas_call x1, Pallas kernels, per_device(): pl.pallas_call(functools.partial(main_kernel, sizes), out_shape=jax.Shape...  28.1 us
    pallas_call x1, Pallas kernels, per_device(): pl.pallas_call(functools.partial(spread_kernel, (wx, drives, rows, wz)),...  3.13 us

profile of v2, /device:TPU:0, one launch (start us, length us, event | category | flops | bytes accessed | tf_op | source)
XLA Modules:
  0.0 31.3 jit_solution(16998348404725223831)
XLA Ops:
  0.0 28.1 %steps.1.dense_hbm = f32[8,8,1024]{2,1,0:T(8,128)} custom-call(f32[4096,16]{1,0:T(8,128)} %bitcast.7, f32[1536,16]{1,0:T(8,128)} %bitcast.8, f32[512,16]{1,0:T(8,128)} %bitcast.9, bf16[4,1024,1024]{2,1,0:T(8,128)(2,1)} %tiles.1, s32[1,1,1,2,4]{4,3,2,1,0:T(2,128)} %bitcast.10, s32[1,1,1,2,4]{4,3,2,1,0:T(2,128)} %bitcast.11, s32[1,1,1,2,4]{4,3,2,1,0:T(2,128)} %bitcast.12, ...), custom_call_target="tpu_custom_call" | custom-call | tf_op jit(solution)/shard_map/steps/pallas_call | solution.py:241
  28.1 3.1 %spread.1 = f32[4096,16]{1,0:T(8,128)} custom-call(f32[8,8,1024]{2,1,0:T(8,128)} %steps.1.dense_hbm), custom_call_target="tpu_custom_call" | custom-call | tf_op jit(solution)/shard_map/spread/pallas_call | solution.py:281

commit v3 on v2

--- a/solution.py
+++ b/solution.py
@@ -25,6 +25,8 @@
     pieces = length // LANES
     per = LANES // wz
     halves = wy // per
+    chunks = p_in.shape[1]
+    wide = length // chunks
     mx, my, mz = lax.axis_index("kx"), lax.axis_index("ky"), lax.axis_index("kz")
 
     def around(me, size, by):
@@ -68,21 +70,25 @@
     in_flight = []
     for it in range(ITERS):
         cur = ext.at[it]
-        waits_p = []
+        waits_p = [[] for _ in range(chunks)]
         for k in range(n_z - 1, -1, -1):
             peer = around(mz, n_z, k)
             blocks = jnp.concatenate(
                 [mid[send_planes[0, 0, 0, c, peer]] for c in range(cap)], axis=0).astype(jnp.bfloat16)
-            if k == 0:
-                p_in[it, 0:cap * drives, :] = blocks
-            else:
-                p_out[it, k * cap * drives:(k + 1) * cap * drives, :] = blocks
-                part = pl.ds(k * cap * drives, cap * drives)
-                copy = pltpu.make_async_remote_copy(
-                    p_out.at[it, part], p_in.at[it, part], p_send.at[it, k], p_recv.at[it, k],
-                    device_id={"kz": peer}, device_id_type=MESH)
+            part = pl.ds(k * cap * drives, cap * drives)
+            for q in range(chunks):
+                piece = blocks[:, q * wide:(q + 1) * wide]
+                if k == 0:
+                    p_in[it, q, 0:cap * drives, :] = piece
+                else:
+                    p_out[it, q, k * cap * drives:(k + 1) * cap * drives, :] = piece
+                    waits_p[q].append(pltpu.make_async_remote_copy(
+                        p_out.at[it, q, part], p_in.at[it, q, part], p_send.at[it, q, k], p_recv.at[it, q, k],
+                        device_id={"kz": peer}, device_id_type=MESH))
+        early = (chunks + 1) // 2
+        for q in range(early):
+            for copy in waits_p[q]:
                 copy.start()
-                waits_p.append(copy)
         waits_h = [
             pltpu.make_async_remote_copy(
                 cur.at[wx:wx + 2], cur.at[0:2], x_send.at[it, 0], x_recv.at[it, 0],
@@ -93,31 +99,33 @@
         for copy in waits_h:
             copy.start()
 
-        def pack(x, carry):
-            part = [cur[x + 2, :, v * LANES:(v + 1) * LANES] for v in range(pieces)]
-            up_z = jnp.zeros((drives, LANES), jnp.float32)
-            down_z = up_z
-            for v in range(pieces):
-                c = part[v]
-                last = jnp.where(z_of == wz - 2, c - 8.0 * roll(c, -1), c)
-                first = jnp.where(z_of == 0, -c, 8.0 * roll(c, 1) - c)
-                here = lax.div(z_of, 2) == v
-                up_z = jnp.where(here, roll(last, 2 * v - (wz - 2)), up_z)
-                down_z = jnp.where(here, roll(first, 2 * v), down_z)
-            z_out[it, 0, x] = up_z
-            z_out[it, 1, x] = down_z
-            up_y = jnp.zeros((drives, LANES), jnp.float32)
-            down_y = up_y
-            width = 2 * wz
-            for b in range(bands):
-                here = lax.div(lane, width) == b
-                up_y = jnp.where(here, roll(part[b * halves + halves - 1], width * b - (LANES - width)), up_y)
-                down_y = jnp.where(here, roll(part[b * halves], width * b), down_y)
-            y_out[it, 0, x] = up_y
-            y_out[it, 1, x] = down_y
-            return carry
-
-        lax.fori_loop(0, wx, pack, 0)
+        width = 2 * wz
+        for x0 in range(0, wx, 2):
+            ups, downs = [], []
+            for x in (x0, x0 + 1):
+                part = [cur[x + 2, :, v * LANES:(v + 1) * LANES] for v in range(pieces)]
+                up_z = jnp.zeros((drives, LANES), jnp.float32)
+                down_z = up_z
+                for v in range(pieces):
+                    c = part[v]
+                    last = jnp.where(z_of == wz - 2, c - 8.0 * roll(c, -1), c)
+                    first = jnp.where(z_of == 0, -c, 8.0 * roll(c, 1) - c)
+                    here = lax.div(z_of, 2) == v
+                    up_z = jnp.where(here, roll(last, 2 * v - (wz - 2)), up_z)
+                    down_z = jnp.where(here, roll(first, 2 * v), down_z)
+                ups.append(up_z)
+                downs.append(down_z)
+                up_y = jnp.zeros((drives, LANES), jnp.float32)
+                down_y = up_y
+                for b in range(bands):
+                    here = lax.div(lane, width) == b
+                    up_y = jnp.where(here, roll(part[b * halves + halves - 1], width * b - (LANES - width)), up_y)
+                    down_y = jnp.where(here, roll(part[b * halves], width * b), down_y)
+                y_out[it, 0, x] = up_y
+                y_out[it, 1, x] = down_y
+            z_out[it, 0, x0 * drives:(x0 + 2) * drives] = jnp.concatenate(ups, axis=0).astype(jnp.bfloat16)
+            z_out[it, 1, x0 * drives:(x0 + 2) * drives] = jnp.concatenate(downs, axis=0).astype(jnp.bfloat16)
+
         for name, me, size, o, i, ss, rs in (("kz", mz, n_z, z_out, z_in, z_send, z_recv), ("ky", my, n_y, y_out, y_in, y_send, y_recv)):
             for way in range(2):
                 copy = pltpu.make_async_remote_copy(
@@ -125,6 +133,9 @@
                     device_id={name: around(me, size, 1 if way == 0 else -1)}, device_id_type=MESH)
                 copy.start()
                 waits_h.append(copy)
+        for q in range(early, chunks):
+            for copy in waits_p[q]:
+                copy.start()
 
         if it == 0:
             for load in loads[1:]:
@@ -156,52 +167,57 @@
         for copy in waits_h:
             copy.wait_recv()
 
-        def step(x, carry):
-            zp, zn = z_in[it, 0, x], z_in[it, 1, x]
-            yp, yn = y_in[it, 0, x], y_in[it, 1, x]
-            width = 2 * wz
-            part = [cur[x + 2, :, v * LANES:(v + 1) * LANES] for v in range(pieces)]
-            for v in range(pieces):
-                at = slice(v * LANES, (v + 1) * LANES)
-                b, h = divmod(v, halves)
-                c = part[v]
-                dx = 8.0 * (cur[x + 3, :, at] - cur[x + 1, :, at]) - (cur[x + 4, :, at] - cur[x, :, at])
-                after = part[v + 1] if h < halves - 1 else roll(yn, -width * b)
-                before = part[v - 1] if h > 0 else roll(yp, LANES - width - width * b)
-                y1 = roll(jnp.where(lane < wz, after, c), -wz)
-                y2 = roll(jnp.where(lane < 2 * wz, after, c), -2 * wz)
-                w1 = roll(jnp.where(lane >= LANES - wz, before, c), wz)
-                w2 = roll(jnp.where(lane >= LANES - 2 * wz, before, c), 2 * wz)
-                dy = 8.0 * (y1 - w1) - (y2 - w2)
-                a1 = jnp.where(z_of < wz - 1, roll(c, -1), 0.0)
-                b1 = jnp.where(z_of >= 1, roll(c, 1), 0.0)
-                a2 = jnp.where(z_of < wz - 2, roll(c, -2), 0.0)
-                b2 = jnp.where(z_of >= 2, roll(c, 2), 0.0)
-                edge = jnp.where(z_of < 2, roll(zp, -2 * v), jnp.where(z_of >= wz - 2, roll(zn, wz - 2 - 2 * v), 0.0))
-                dz = 8.0 * (a1 - b1) - (a2 - b2) + edge
-                fx, fy, fz, r = (field[a, x, :, at] for a in range(4))
-                base[pl.ds(pl.multiple_of(x * drives, drives), drives), at] = c - (fx * dx + fy * dy + fz * dz) - r * c
+        def step(pair_at, carry):
+            both = pl.ds(pl.multiple_of(pair_at * 2 * drives, 2 * drives), 2 * drives)
+            zps, zns = z_in[it, 0, both].astype(jnp.float32), z_in[it, 1, both].astype(jnp.float32)
+            for j in range(2):
+                x = pair_at * 2 + j
+                zp, zn = zps[j * drives:(j + 1) * drives], zns[j * drives:(j + 1) * drives]
+                yp, yn = y_in[it, 0, x], y_in[it, 1, x]
+                part = [cur[x + 2, :, v * LANES:(v + 1) * LANES] for v in range(pieces)]
+                for v in range(pieces):
+                    at = slice(v * LANES, (v + 1) * LANES)
+                    b, h = divmod(v, halves)
+                    c = part[v]
+                    dx = 8.0 * (cur[x + 3, :, at] - cur[x + 1, :, at]) - (cur[x + 4, :, at] - cur[x, :, at])
+                    after = part[v + 1] if h < halves - 1 else roll(yn, -width * b)
+                    before = part[v - 1] if h > 0 else roll(yp, LANES - width - width * b)
+                    y1 = roll(jnp.where(lane < wz, after, c), -wz)
+                    y2 = roll(jnp.where(lane < 2 * wz, after, c), -2 * wz)
+                    w1 = roll(jnp.where(lane >= LANES - wz, before, c), wz)
+                    w2 = roll(jnp.where(lane >= LANES - 2 * wz, before, c), 2 * wz)
+                    dy = 8.0 * (y1 - w1) - (y2 - w2)
+                    a1 = jnp.where(z_of < wz - 1, roll(c, -1), 0.0)
+                    b1 = jnp.where(z_of >= 1, roll(c, 1), 0.0)
+                    a2 = jnp.where(z_of < wz - 2, roll(c, -2), 0.0)
+                    b2 = jnp.where(z_of >= 2, roll(c, 2), 0.0)
+                    edge = jnp.where(z_of < 2, roll(zp, -2 * v), jnp.where(z_of >= wz - 2, roll(zn, wz - 2 - 2 * v), 0.0))
+                    dz = 8.0 * (a1 - b1) - (a2 - b2) + edge
+                    fx, fy, fz, r = (field[a, x, :, at] for a in range(4))
+                    base[pl.ds(pl.multiple_of(x * drives, drives), drives), at] = c - (fx * dx + fy * dy + fz * dz) - r * c
             return carry
 
-        lax.fori_loop(0, wx, step, 0)
-
-        for copy in waits_p:
-            copy.wait_recv()
-        grouped = jnp.dot(sel, p_in[it], preferred_element_type=jnp.float32).astype(jnp.bfloat16)
+        lax.fori_loop(0, wx // 2, step, 0)
+
         m = wx * drives
         total = base[...]
-        for t in range(n_tiles):
-            if it == 0:
-                tile_loads[t].wait()
-            total = total + lax.dot_general(
-                grouped[t * m:(t + 1) * m], tiles_in[t], (((1,), (1,)), ((), ())), preferred_element_type=jnp.float32)
+        for q in range(chunks):
+            for copy in waits_p[q]:
+                copy.wait_recv()
+            grouped = jnp.dot(sel, p_in[it, q], preferred_element_type=jnp.float32).astype(jnp.bfloat16)
+            for t in range(n_tiles):
+                if it == 0 and q == 0:
+                    tile_loads[t].wait()
+                total = total + lax.dot_general(
+                    grouped[t * m:(t + 1) * m], tiles_in[t, :, q * wide:(q + 1) * wide],
+                    (((1,), (1,)), ((), ())), preferred_element_type=jnp.float32)
         total = total.reshape(wx, drives, length)
         if it == ITERS - 1:
             out[...] = total
         else:
             ext[it + 1, 2:wx + 2] = total
             mid[...] = total
-        in_flight += waits_p + waits_h
+        in_flight += sum(waits_p, []) + waits_h
     for copy in in_flight:
         copy.wait_send()
 
@@ -235,6 +251,7 @@
     rows = bands * wy
     sizes = (n_x, n_y, n_z, wx, drives, bands, wy, wz, cap, n_tiles)
     vmem = pl.BlockSpec(memory_space=pltpu.VMEM)
+    chunks = bands if n_z <= 8 else 1
     hbm = pl.BlockSpec(memory_space=pltpu.HBM)
     f32, b16 = jnp.float32, jnp.bfloat16
     dma = pltpu.SemaphoreType.DMA
@@ -258,13 +275,13 @@
             pltpu.VMEM((wx * drives, length), f32),
             pltpu.VMEM((ITERS, 2, wx, drives, LANES), f32),
             pltpu.VMEM((ITERS, 2, wx, drives, LANES), f32),
-            pltpu.VMEM((ITERS, 2, wx, drives, LANES), f32),
-            pltpu.VMEM((ITERS, 2, wx, drives, LANES), f32),
-            pltpu.VMEM((ITERS, n_z * cap * drives, length), b16),
-            pltpu.VMEM((ITERS, n_z * cap * drives, length), b16),
+            pltpu.VMEM((ITERS, 2, wx * drives, LANES), b16),
+            pltpu.VMEM((ITERS, 2, wx * drives, LANES), b16),
+            pltpu.VMEM((ITERS, chunks, n_z * cap * drives, length // chunks), b16),
+            pltpu.VMEM((ITERS, chunks, n_z * cap * drives, length // chunks), b16),
             dma((6,)), dma((wx,)), dma((n_tiles,)),
             dma((ITERS, 2)), dma((ITERS, 2)), dma((ITERS, 2)), dma((ITERS, 2)), dma((ITERS, 2)), dma((ITERS, 2)),
-            dma((ITERS, n_z)), dma((ITERS, n_z)),
+            dma((ITERS, chunks, n_z)), dma((ITERS, chunks, n_z)),
         ],
         compiler_params=pltpu.CompilerParams(collective_id=0, has_side_effects=True, vmem_limit_bytes=60 * 2**20),
         name="steps",

time: 31.5 us -> 31.4 us (level)
  no operation moved by 1% of the time
where the time goes in v3:
time: 31.4 us; the launch traced here: 31.2 us
  Pallas kernels  31.2 us (99%)
    pallas_call x1, Pallas kernels, per_device(): pl.pallas_call(functools.partial(main_kernel, sizes), out_shape=jax.Shape...  28.1 us
    pallas_call x1, Pallas kernels, per_device(): pl.pallas_call(functools.partial(spread_kernel, (wx, drives, rows, wz)),...  3.13 us

profile of v3, /device:TPU:0, one launch (start us, length us, event | category | flops | bytes accessed | tf_op | source)
XLA Modules:
  0.0 31.2 jit_solution(17503424562813209396)
XLA Ops:
  0.0 28.1 %steps.1.dense_hbm = f32[8,8,1024]{2,1,0:T(8,128)} custom-call(f32[4096,16]{1,0:T(8,128)} %bitcast.7, f32[1536,16]{1,0:T(8,128)} %bitcast.8, f32[512,16]{1,0:T(8,128)} %bitcast.9, bf16[4,1024,1024]{2,1,0:T(8,128)(2,1)} %tiles.1, s32[1,1,1,2,4]{4,3,2,1,0:T(2,128)} %bitcast.10, s32[1,1,1,2,4]{4,3,2,1,0:T(2,128)} %bitcast.11, s32[1,1,1,2,4]{4,3,2,1,0:T(2,128)} %bitcast.12, ...), custom_call_target="tpu_custom_call" | custom-call | tf_op jit(solution)/shard_map/steps/pallas_call | solution.py:258
  28.1 3.1 %spread.1 = f32[4096,16]{1,0:T(8,128)} custom-call(f32[8,8,1024]{2,1,0:T(8,128)} %steps.1.dense_hbm), custom_call_target="tpu_custom_call" | custom-call | tf_op jit(solution)/shard_map/spread/pallas_call | solution.py:298

commit v4 on v3

--- a/solution.py
+++ b/solution.py
@@ -17,7 +17,7 @@
 
 
 def main_kernel(sizes, pop, force, rate, tiles, send_hbm, target_hbm, tile_hbm, count_hbm, out,
-                send_planes, recv_target, recv_tile, recv_count, pop_in, force_in, rate_in, tiles_in, ext, mid, field, base, y_out, y_in, z_out, z_in,
+                send_planes, recv_target, recv_tile, recv_count, pop_in, force_in, rate_in, tiles_in, ext, mid, field, sel, base, y_out, y_in, z_out, z_in,
                 p_out, p_in, in_sem, pop_sem, tile_sem, x_send, x_recv, y_send, y_recv, z_send, z_recv, p_send, p_recv):
     n_x, n_y, n_z, wx, drives, bands, wy, wz, cap, n_tiles = sizes
     rows = bands * wy
@@ -41,10 +41,13 @@
         pl.semaphore_signal(barrier, inc=1, device_id=friend, device_id_type=MESH)
 
     pop_rows = drives * rows
-    pop_loads = [pltpu.make_async_copy(pop.at[pl.ds(x * pop_rows, pop_rows)], pop_in.at[pl.ds(x * pop_rows, pop_rows)], pop_sem.at[x])
-                 for x in range(wx)]
-    for load in pop_loads:
-        load.start()
+
+    def pop_load(x):
+        part = pl.ds(pl.multiple_of(x * pop_rows, 8), pop_rows)
+        return pltpu.make_async_copy(pop.at[part], pop_in.at[part], pop_sem.at[x])
+
+    for x in range(wx):
+        pop_load(x).start()
     pairs = ((send_hbm, send_planes), (target_hbm, recv_target), (tile_hbm, recv_tile), (count_hbm, recv_count), (force, force_in), (rate, rate_in))
     loads = [pltpu.make_async_copy(a, b, in_sem.at[i]) for i, (a, b) in enumerate(pairs)]
     for load in loads:
@@ -56,53 +59,71 @@
     lane = lax.broadcasted_iota(jnp.int32, (8, LANES), 1)
     z_of = lax.rem(lane, wz)
 
-    for x in range(wx):
-        pop_loads[x].wait()
+    def lay_pop(x, carry):
+        pop_load(x).wait()
         for v in range(pieces):
             piece = jnp.concatenate(
                 [pop_in[pl.ds(x * pop_rows + v * per + i, drives, stride=rows), :] for i in range(per)], axis=1)
             ext[0, x + 2, :, v * LANES:(v + 1) * LANES] = piece
             mid[x, :, v * LANES:(v + 1) * LANES] = piece
+        return carry
+
+    lax.fori_loop(0, wx, lay_pop, 0)
     loads[0].wait()
     pl.semaphore_wait(barrier, len(friends))
 
-    sel = None
-    in_flight = []
-    for it in range(ITERS):
+    early = (chunks + 1) // 2
+    width = 2 * wz
+    m = wx * drives
+
+    def plane_copies(it, q):
+        copies = []
+        for k in range(n_z - 1, 0, -1):
+            part = pl.ds(k * cap * drives, cap * drives)
+            copies.append(pltpu.make_async_remote_copy(
+                p_out.at[it, q, part], p_in.at[it, q, part], p_send.at[it, q, k], p_recv.at[it, q, k],
+                device_id={"kz": around(mz, n_z, k)}, device_id_type=MESH))
+        return copies
+
+    def x_copies(it):
         cur = ext.at[it]
-        waits_p = [[] for _ in range(chunks)]
-        for k in range(n_z - 1, -1, -1):
-            peer = around(mz, n_z, k)
-            blocks = jnp.concatenate(
-                [mid[send_planes[0, 0, 0, c, peer]] for c in range(cap)], axis=0).astype(jnp.bfloat16)
-            part = pl.ds(k * cap * drives, cap * drives)
-            for q in range(chunks):
-                piece = blocks[:, q * wide:(q + 1) * wide]
-                if k == 0:
-                    p_in[it, q, 0:cap * drives, :] = piece
-                else:
-                    p_out[it, q, k * cap * drives:(k + 1) * cap * drives, :] = piece
-                    waits_p[q].append(pltpu.make_async_remote_copy(
-                        p_out.at[it, q, part], p_in.at[it, q, part], p_send.at[it, q, k], p_recv.at[it, q, k],
-                        device_id={"kz": peer}, device_id_type=MESH))
-        early = (chunks + 1) // 2
-        for q in range(early):
-            for copy in waits_p[q]:
-                copy.start()
-        waits_h = [
+        return [
             pltpu.make_async_remote_copy(
                 cur.at[wx:wx + 2], cur.at[0:2], x_send.at[it, 0], x_recv.at[it, 0],
                 device_id={"kx": around(mx, n_x, 1)}, device_id_type=MESH),
             pltpu.make_async_remote_copy(
                 cur.at[2:4], cur.at[wx + 2:wx + 4], x_send.at[it, 1], x_recv.at[it, 1],
                 device_id={"kx": around(mx, n_x, -1)}, device_id_type=MESH)]
-        for copy in waits_h:
+
+    def edge_copies(it):
+        copies = []
+        for name, me, size, o, i, ss, rs in (("kz", mz, n_z, z_out, z_in, z_send, z_recv), ("ky", my, n_y, y_out, y_in, y_send, y_recv)):
+            for way in range(2):
+                copies.append(pltpu.make_async_remote_copy(
+                    o.at[it, way], i.at[it, way], ss.at[it, way], rs.at[it, way],
+                    device_id={name: around(me, size, 1 if way == 0 else -1)}, device_id_type=MESH))
+        return copies
+
+    def time_step(it, carry):
+        cur = ext.at[it]
+        for copy in x_copies(it):
             copy.start()
-
-        width = 2 * wz
-        for x0 in range(0, wx, 2):
+        for k in range(n_z - 1, -1, -1):
+            peer = around(mz, n_z, k)
+            blocks = jnp.concatenate(
+                [mid[send_planes[0, 0, 0, c, peer]] for c in range(cap)], axis=0).astype(jnp.bfloat16)
+            to = p_in if k == 0 else p_out
+            for q in range(chunks):
+                to[it, q, k * cap * drives:(k + 1) * cap * drives, :] = blocks[:, q * wide:(q + 1) * wide]
+        for q in range(early):
+            for copy in plane_copies(it, q):
+                copy.start()
+
+        def pack(pair_at, carry):
+            both = pl.ds(pl.multiple_of(pair_at * 2 * drives, 2 * drives), 2 * drives)
             ups, downs = [], []
-            for x in (x0, x0 + 1):
+            for j in range(2):
+                x = pair_at * 2 + j
                 part = [cur[x + 2, :, v * LANES:(v + 1) * LANES] for v in range(pieces)]
                 up_z = jnp.zeros((drives, LANES), jnp.float32)
                 down_z = up_z
@@ -123,25 +144,24 @@
                     down_y = jnp.where(here, roll(part[b * halves], width * b), down_y)
                 y_out[it, 0, x] = up_y
                 y_out[it, 1, x] = down_y
-            z_out[it, 0, x0 * drives:(x0 + 2) * drives] = jnp.concatenate(ups, axis=0).astype(jnp.bfloat16)
-            z_out[it, 1, x0 * drives:(x0 + 2) * drives] = jnp.concatenate(downs, axis=0).astype(jnp.bfloat16)
-
-        for name, me, size, o, i, ss, rs in (("kz", mz, n_z, z_out, z_in, z_send, z_recv), ("ky", my, n_y, y_out, y_in, y_send, y_recv)):
-            for way in range(2):
-                copy = pltpu.make_async_remote_copy(
-                    o.at[it, way], i.at[it, way], ss.at[it, way], rs.at[it, way],
-                    device_id={name: around(me, size, 1 if way == 0 else -1)}, device_id_type=MESH)
+            z_out[it, 0, both] = jnp.concatenate(ups, axis=0).astype(jnp.bfloat16)
+            z_out[it, 1, both] = jnp.concatenate(downs, axis=0).astype(jnp.bfloat16)
+            return carry
+
+        lax.fori_loop(0, wx // 2, pack, 0)
+        for copy in edge_copies(it):
+            copy.start()
+        for q in range(early, chunks):
+            for copy in plane_copies(it, q):
                 copy.start()
-                waits_h.append(copy)
-        for q in range(early, chunks):
-            for copy in waits_p[q]:
-                copy.start()
-
-        if it == 0:
+
+        @pl.when(it == 0)
+        def _():
             for load in loads[1:]:
                 load.wait()
-            for v in range(pieces):
-                at = slice(v * LANES, (v + 1) * LANES)
+
+            def lay_field(v, carry):
+                at = pl.ds(pl.multiple_of(v * LANES, LANES), LANES)
                 for a in range(4):
                     source, first, stride = (force_in, a * rows, 3 * rows) if a < 3 else (rate_in, 0, rows)
                     piece = jnp.concatenate(
@@ -150,6 +170,9 @@
                         piece = piece * (1.0 / 12.0)
                     for x in range(wx):
                         field[a, x, :, at] = jnp.broadcast_to(piece[x:x + 1], (drives, LANES))
+                return carry
+
+            lax.fori_loop(0, pieces, lay_field, 0)
             slots = n_z * cap
             col = lax.broadcasted_iota(jnp.int32, (8, slots * drives), 1)
             pair = jnp.full((8, slots * drives), -1, jnp.int32)
@@ -159,12 +182,12 @@
                 for c in range(cap):
                     code = jnp.where(c < count, recv_tile[0, 0, 0, c, source] * wx + recv_target[0, 0, 0, c, source], -1)
                     pair = jnp.where(lax.div(col, drives) == k * cap + c, code, pair)
-            row = lax.broadcasted_iota(jnp.int32, (n_tiles * wx * drives, slots * drives), 0)
-            col = lax.broadcasted_iota(jnp.int32, (n_tiles * wx * drives, slots * drives), 1)
+            row = lax.broadcasted_iota(jnp.int32, (n_tiles * m, slots * drives), 0)
+            col = lax.broadcasted_iota(jnp.int32, (n_tiles * m, slots * drives), 1)
             hit = (lax.div(row, drives) == pair[0:1]) & (lax.rem(row, drives) == lax.rem(col, drives))
-            sel = jnp.where(hit, 1.0, 0.0).astype(jnp.bfloat16)
-
-        for copy in waits_h:
+            sel[...] = jnp.where(hit, 1.0, 0.0).astype(jnp.bfloat16)
+
+        for copy in x_copies(it) + edge_copies(it):
             copy.wait_recv()
 
         def step(pair_at, carry):
@@ -199,48 +222,73 @@
 
         lax.fori_loop(0, wx // 2, step, 0)
 
-        m = wx * drives
-        total = base[...]
+        @pl.when(it == 0)
+        def _():
+            for load in tile_loads:
+                load.wait()
+
+        def product(q, carry):
+            for copy in plane_copies(it, q):
+                copy.wait_recv()
+            at = pl.ds(pl.multiple_of(q * wide, LANES), wide)
+            grouped = jnp.dot(sel[...], p_in[it, q], preferred_element_type=jnp.float32).astype(jnp.bfloat16)
+            total = base[...]
+            for t in range(n_tiles):
+                total = total + lax.dot_general(
+                    grouped[t * m:(t + 1) * m], tiles_in[t, :, at],
+                    (((1,), (1,)), ((), ())), preferred_element_type=jnp.float32)
+            base[...] = total
+            return carry
+
+        lax.fori_loop(0, chunks, product, 0)
+        total = base[...].reshape(wx, drives, length)
+        ext[it + 1, 2:wx + 2] = total
+        mid[...] = total
+        return carry
+
+    lax.fori_loop(0, ITERS, time_step, 0)
+    result = pltpu.make_async_copy(mid, out, in_sem.at[0])
+    result.start()
+
+    def drain(it, carry):
+        for copy in x_copies(it) + edge_copies(it):
+            copy.wait_send()
         for q in range(chunks):
-            for copy in waits_p[q]:
-                copy.wait_recv()
-            grouped = jnp.dot(sel, p_in[it, q], preferred_element_type=jnp.float32).astype(jnp.bfloat16)
-            for t in range(n_tiles):
-                if it == 0 and q == 0:
-                    tile_loads[t].wait()
-                total = total + lax.dot_general(
-                    grouped[t * m:(t + 1) * m], tiles_in[t, :, q * wide:(q + 1) * wide],
-                    (((1,), (1,)), ((), ())), preferred_element_type=jnp.float32)
-        total = total.reshape(wx, drives, length)
-        if it == ITERS - 1:
-            out[...] = total
-        else:
-            ext[it + 1, 2:wx + 2] = total
-            mid[...] = total
-        in_flight += sum(waits_p, []) + waits_h
-    for copy in in_flight:
-        copy.wait_send()
+            for copy in plane_copies(it, q):
+                copy.wait_send()
+        return carry
+
+    lax.fori_loop(0, ITERS, drain, 0)
+    result.wait()
 
 
 def spread_kernel(sizes, dense_hbm, out, dense, laid, in_sem, sem):
     wx, drives, rows, wz = sizes
     per = LANES // wz
     pieces = rows // per
-    loads = [pltpu.make_async_copy(dense_hbm.at[x], dense.at[x], in_sem.at[x]) for x in range(wx)]
-    for load in loads:
-        load.start()
-    copies = []
+
+    def load(x):
+        return pltpu.make_async_copy(dense_hbm.at[x], dense.at[x], in_sem.at[x])
+
+    def store(x):
+        part = pl.ds(pl.multiple_of(x * drives * rows, 8), drives * rows)
+        return pltpu.make_async_copy(laid.at[part], out.at[part], sem.at[x])
+
     for x in range(wx):
-        loads[x].wait()
+        load(x).start()
+
+    def lay(x, carry):
+        load(x).wait()
         for v in range(pieces):
             piece = dense[x, :, v * LANES:(v + 1) * LANES]
             for i in range(per):
                 laid[pl.ds(x * drives * rows + v * per + i, drives, stride=rows), :] = roll(piece, -i * wz)[:, :wz]
-        part = pl.ds(x * drives * rows, drives * rows)
-        copies.append(pltpu.make_async_copy(laid.at[part], out.at[part], sem.at[x]))
-        copies[-1].start()
-    for copy in copies:
-        copy.wait()
+        store(x).start()
+        return carry
+
+    lax.fori_loop(0, wx, lay, 0)
+    for x in range(wx):
+        store(x).wait()
 
 
 def per_device(mesh_shape, populations, force, rate, tiles, send_planes, recv_target, recv_tile, recv_count):
@@ -250,7 +298,6 @@
     n_x, n_y, n_z = mesh_shape
     rows = bands * wy
     sizes = (n_x, n_y, n_z, wx, drives, bands, wy, wz, cap, n_tiles)
-    vmem = pl.BlockSpec(memory_space=pltpu.VMEM)
     chunks = bands if n_z <= 8 else 1
     hbm = pl.BlockSpec(memory_space=pltpu.HBM)
     f32, b16 = jnp.float32, jnp.bfloat16
@@ -259,7 +306,7 @@
         functools.partial(main_kernel, sizes),
         out_shape=jax.ShapeDtypeStruct((wx, drives, length), f32),
         in_specs=[hbm] * 8,
-        out_specs=vmem,
+        out_specs=hbm,
         scratch_shapes=[
             pltpu.SMEM((1, 1, 1, cap, n_z), jnp.int32),
             pltpu.SMEM((1, 1, 1, cap, n_z), jnp.int32),
@@ -269,9 +316,10 @@
             pltpu.VMEM((wx * 3 * rows, wz), f32),
             pltpu.VMEM((wx * rows, wz), f32),
             pltpu.VMEM(tiles.shape, b16),
-            pltpu.VMEM((ITERS, wx + 4, drives, length), f32),
+            pltpu.VMEM((ITERS + 1, wx + 4, drives, length), f32),
             pltpu.VMEM((wx, drives, length), f32),
             pltpu.VMEM((4, wx, drives, length), f32),
+            pltpu.VMEM((n_tiles * wx * drives, n_z * cap * drives), b16),
             pltpu.VMEM((wx * drives, length), f32),
             pltpu.VMEM((ITERS, 2, wx, drives, LANES), f32),
             pltpu.VMEM((ITERS, 2, wx, drives, LANES), f32),

time: 31.4 us -> 32.2 us (1.025)
  Pallas kernels: 31.2 us -> 32 us
    pallas_call x1, Pallas kernels: 28.1 us -> 28.9 us  [per_device(): pl.pallas_call(functools.partial(main_kernel, sizes), out_shape=jax.Shape...]
where the time goes in v4:
time: 32.2 us; the launch traced here: 32 us
  Pallas kernels  32 us (99%)
    pallas_call x1, Pallas kernels, per_device(): pl.pallas_call(functools.partial(main_kernel, sizes), out_shape=jax.Shape...  28.9 us
    pallas_call x1, Pallas kernels, per_device(): pl.pallas_call(functools.partial(spread_kernel, (wx, drives, rows, wz)),...  3.1 us

profile of v4, /device:TPU:0, one launch (start us, length us, event | category | flops | bytes accessed | tf_op | source)
XLA Modules:
  0.0 32.0 jit_solution(17578026817593019251)
XLA Ops:
  0.0 28.9 %steps.1.dense_hbm = f32[8,8,1024]{2,1,0:T(8,128)} custom-call(f32[4096,16]{1,0:T(8,128)} %bitcast.7, f32[1536,16]{1,0:T(8,128)} %bitcast.8, f32[512,16]{1,0:T(8,128)} %bitcast.9, bf16[4,1024,1024]{2,1,0:T(8,128)(2,1)} %tiles.1, s32[1,1,1,2,4]{4,3,2,1,0:T(2,128)} %bitcast.10, s32[1,1,1,2,4]{4,3,2,1,0:T(2,128)} %bitcast.11, s32[1,1,1,2,4]{4,3,2,1,0:T(2,128)} %bitcast.12, ...), custom_call_target="tpu_custom_call" | custom-call | tf_op jit(solution)/shard_map/steps/pallas_call | solution.py:305
  28.9 3.1 %spread.1 = f32[4096,16]{1,0:T(8,128)} custom-call(f32[8,8,1024]{2,1,0:T(8,128)} %steps.1.dense_hbm), custom_call_target="tpu_custom_call" | custom-call | tf_op jit(solution)/shard_map/spread/pallas_call | solution.py:346

commit v5 on v4

--- a/solution.py
+++ b/solution.py
@@ -17,7 +17,7 @@
 
 
 def main_kernel(sizes, pop, force, rate, tiles, send_hbm, target_hbm, tile_hbm, count_hbm, out,
-                send_planes, recv_target, recv_tile, recv_count, pop_in, force_in, rate_in, tiles_in, ext, mid, field, sel, base, y_out, y_in, z_out, z_in,
+                send_planes, recv_target, recv_tile, recv_count, pop_in, force_in, rate_in, tiles_in, ext, mid, field, sel, turned, base, y_out, y_in, z_out, z_in,
                 p_out, p_in, in_sem, pop_sem, tile_sem, x_send, x_recv, y_send, y_recv, z_send, z_recv, p_send, p_recv):
     n_x, n_y, n_z, wx, drives, bands, wy, wz, cap, n_tiles = sizes
     rows = bands * wy
@@ -232,15 +232,18 @@
                 copy.wait_recv()
             at = pl.ds(pl.multiple_of(q * wide, LANES), wide)
             grouped = jnp.dot(sel[...], p_in[it, q], preferred_element_type=jnp.float32).astype(jnp.bfloat16)
-            total = base[...]
+            total = None
             for t in range(n_tiles):
-                total = total + lax.dot_general(
-                    grouped[t * m:(t + 1) * m], tiles_in[t, :, at],
+                term = lax.dot_general(
+                    tiles_in[t, :, at], grouped[t * m:(t + 1) * m],
                     (((1,), (1,)), ((), ())), preferred_element_type=jnp.float32)
-            base[...] = total
+                total = term if total is None else total + term
+            turned[...] += total
             return carry
 
+        turned[...] = jnp.zeros_like(turned)
         lax.fori_loop(0, chunks, product, 0)
+        base[...] += jnp.transpose(turned[...])
         total = base[...].reshape(wx, drives, length)
         ext[it + 1, 2:wx + 2] = total
         mid[...] = total
@@ -320,6 +323,7 @@
             pltpu.VMEM((wx, drives, length), f32),
             pltpu.VMEM((4, wx, drives, length), f32),
             pltpu.VMEM((n_tiles * wx * drives, n_z * cap * drives), b16),
+            pltpu.VMEM((length, wx * drives), f32),
             pltpu.VMEM((wx * drives, length), f32),
             pltpu.VMEM((ITERS, 2, wx, drives, LANES), f32),
             pltpu.VMEM((ITERS, 2, wx, drives, LANES), f32),

time: 32.2 us -> 32.8 us (1.019)
  Pallas kernels: 32 us -> 32.6 us
    pallas_call x1, Pallas kernels: 28.9 us -> 29.5 us  [per_device(): pl.pallas_call(functools.partial(main_kernel, sizes), out_shape=jax.Shape...]
where the time goes in v5:
time: 32.8 us; the launch traced here: 32.6 us
  Pallas kernels  32.6 us (99%)
    pallas_call x1, Pallas kernels, per_device(): pl.pallas_call(functools.partial(main_kernel, sizes), out_shape=jax.Shape...  29.5 us
    pallas_call x1, Pallas kernels, per_device(): pl.pallas_call(functools.partial(spread_kernel, (wx, drives, rows, wz)),...  3.1 us

profile of v5, /device:TPU:0, one launch (start us, length us, event | category | flops | bytes accessed | tf_op | source)
XLA Modules:
  0.0 32.6 jit_solution(15427818421160697393)
XLA Ops:
  0.0 29.5 %steps.1.dense_hbm = f32[8,8,1024]{2,1,0:T(8,128)} custom-call(f32[4096,16]{1,0:T(8,128)} %bitcast.7, f32[1536,16]{1,0:T(8,128)} %bitcast.8, f32[512,16]{1,0:T(8,128)} %bitcast.9, bf16[4,1024,1024]{2,1,0:T(8,128)(2,1)} %tiles.1, s32[1,1,1,2,4]{4,3,2,1,0:T(2,128)} %bitcast.10, s32[1,1,1,2,4]{4,3,2,1,0:T(2,128)} %bitcast.11, s32[1,1,1,2,4]{4,3,2,1,0:T(2,128)} %bitcast.12, ...), custom_call_target="tpu_custom_call" | custom-call | tf_op jit(solution)/shard_map/steps/pallas_call | solution.py:308
  29.5 3.1 %spread.1 = f32[4096,16]{1,0:T(8,128)} custom-call(f32[8,8,1024]{2,1,0:T(8,128)} %steps.1.dense_hbm), custom_call_target="tpu_custom_call" | custom-call | tf_op jit(solution)/shard_map/spread/pallas_call | solution.py:350

commit v6 on v3

--- a/solution.py
+++ b/solution.py
@@ -50,8 +50,6 @@
     for load in loads:
         load.start()
     tile_loads = [pltpu.make_async_copy(tiles.at[t], tiles_in.at[t], tile_sem.at[t]) for t in range(n_tiles)]
-    for load in tile_loads:
-        load.start()
 
     lane = lax.broadcasted_iota(jnp.int32, (8, LANES), 1)
     z_of = lax.rem(lane, wz)
@@ -63,6 +61,8 @@
                 [pop_in[pl.ds(x * pop_rows + v * per + i, drives, stride=rows), :] for i in range(per)], axis=1)
             ext[0, x + 2, :, v * LANES:(v + 1) * LANES] = piece
             mid[x, :, v * LANES:(v + 1) * LANES] = piece
+    for load in tile_loads:
+        load.start()
     loads[0].wait()
     pl.semaphore_wait(barrier, len(friends))
 
@@ -251,7 +251,7 @@
     rows = bands * wy
     sizes = (n_x, n_y, n_z, wx, drives, bands, wy, wz, cap, n_tiles)
     vmem = pl.BlockSpec(memory_space=pltpu.VMEM)
-    chunks = bands if n_z <= 8 else 1
+    chunks = 2 if n_z <= 8 else 1
     hbm = pl.BlockSpec(memory_space=pltpu.HBM)
     f32, b16 = jnp.float32, jnp.bfloat16
     dma = pltpu.SemaphoreType.DMA

time: 31.4 us -> 29.9 us (0.952)
  Pallas kernels: 31.2 us -> 29.7 us
    pallas_call x1, Pallas kernels: 28.1 us -> 26.6 us  [per_device(): pl.pallas_call(functools.partial(main_kernel, sizes), out_shape=jax.Shape...]
where the time goes in v6:
time: 29.9 us; the launch traced here: 29.7 us
  Pallas kernels  29.7 us (99%)
    pallas_call x1, Pallas kernels, per_device(): pl.pallas_call(functools.partial(main_kernel, sizes), out_shape=jax.Shape...  26.6 us
    pallas_call x1, Pallas kernels, per_device(): pl.pallas_call(functools.partial(spread_kernel, (wx, drives, rows, wz)),...  3.13 us

profile of v6, /device:TPU:0, one launch (start us, length us, event | category | flops | bytes accessed | tf_op | source)
XLA Modules:
  0.0 29.7 jit_solution(3624315648815272783)
XLA Ops:
  0.0 26.6 %steps.1.dense_hbm = f32[8,8,1024]{2,1,0:T(8,128)} custom-call(f32[4096,16]{1,0:T(8,128)} %bitcast.7, f32[1536,16]{1,0:T(8,128)} %bitcast.8, f32[512,16]{1,0:T(8,128)} %bitcast.9, bf16[4,1024,1024]{2,1,0:T(8,128)(2,1)} %tiles.1, s32[1,1,1,2,4]{4,3,2,1,0:T(2,128)} %bitcast.10, s32[1,1,1,2,4]{4,3,2,1,0:T(2,128)} %bitcast.11, s32[1,1,1,2,4]{4,3,2,1,0:T(2,128)} %bitcast.12, ...), custom_call_target="tpu_custom_call" | custom-call | tf_op jit(solution)/shard_map/steps/pallas_call | solution.py:258
  26.6 3.1 %spread.1 = f32[4096,16]{1,0:T(8,128)} custom-call(f32[8,8,1024]{2,1,0:T(8,128)} %steps.1.dense_hbm), custom_call_target="tpu_custom_call" | custom-call | tf_op jit(solution)/shard_map/spread/pallas_call | solution.py:298
